TPU v7x, 32 devices: a whole 2x2x4 slice. The times are simulated.
32 devices in a mesh: fsdp: 4 (over y, x), dp: 8 (over z, core).
Axes of the slice: x: 2, y: 2, z: 4, core: 2. Of those that a mesh axis runs over, the one named last changes fastest.
Arguments:
- noise_embed: bfloat16 [512, 1024], P(('fsdp', 'dp')), may hold values from -6 to 6
- action_embed: bfloat16 [512, 1024], P(('fsdp', 'dp')), may hold values from -6 to 6
- prefix_kv: bfloat16 [2, 32, 256, 256], P(None, ('fsdp', 'dp')), may hold values from -6 to 6
- flow_step: int32 [32], P(('fsdp', 'dp')), may hold values from 0 to 9
- action_mask: int32 [512], P(('fsdp', 'dp')), may hold values 0 or 1
- w_up: bfloat16 [1024, 4096], P(None, 'fsdp'), may hold values from -0.1875 to 0.1875
- w_down: bfloat16 [4096, 1024], P('fsdp'), may hold values from -0.09375 to 0.09375
- query_grad: float32 [1024, 4096], P(None, 'fsdp'), may hold values from -6 to 6
Outputs:
- inverse_hvp: float32 [1024, 4096], P(None, 'fsdp')
- scores: float32 [32], P(('fsdp', 'dp'))
All inputs are finite; a program needn't handle non-finite values. No bound on the sum of `action_mask` on one device may be relied on, other than what follows from the above.
Results may differ from a plain program's by a relative error of at most 0.03.
Values may be sent and summed in bfloat16 or wider, within the bound.
A program may use at most 64 MiB of HBM per device.

v0:
```python
import math

import jax
import jax.numpy as jnp
from jax import lax
from jax.sharding import PartitionSpec as P

D = 1024
FF = 4096
STEPS_T = 10
ITERS = 2


epsilon = 1e-06
sharpness_divisor = 6.0
damping_factor = 0.01


def attend(noise_embed, action_embed, prefix_kv, flow_step):
    demos = flow_step.shape[0]
    acts = noise_embed.shape[0] // demos
    channel_span = prefix_kv.shape[3]
    width = noise_embed.shape[1]
    times = (flow_step.astype(jnp.float32) + 1.0) / (STEPS_T + 1.0)
    per_token = jnp.repeat(times, acts)[:, None]
    noisy = noise_embed.astype(jnp.float32)
    clean = action_embed.astype(jnp.float32)
    inputs = per_token * noisy + (1.0 - per_token) * clean
    target = noisy - clean
    queries = inputs.reshape(demos, acts, width // channel_span, channel_span)
    probe_length = (
        queries * lax.rsqrt(jnp.mean(queries * queries, -1, keepdims=True) + epsilon)
    ).astype(jnp.bfloat16)
    keys = prefix_kv[0].astype(jnp.float32)
    lookup_length = (keys * lax.rsqrt(jnp.mean(keys * keys, -1, keepdims=True) + epsilon)).astype(
        jnp.bfloat16
    )
    match_energies = jnp.einsum(
        "zilf,zgf->zilg", probe_length, lookup_length, preferred_element_type=jnp.float32
    ) * (sharpness_divisor / channel_span)
    expo = jnp.exp(match_energies)
    weights = (expo / jnp.sum(expo, -1, keepdims=True)).astype(jnp.bfloat16)
    mixed = jnp.einsum("dahp,dpe->dahe", weights, prefix_kv[1], preferred_element_type=jnp.float32)
    hidden = inputs + mixed.reshape(demos * acts, width)
    normed_rows = (
        hidden * lax.rsqrt(jnp.mean(hidden * hidden, -1, keepdims=True) + epsilon)
    ).astype(jnp.bfloat16)
    return (hidden, normed_rows, target, acts)


def down_rows(source, w_down):
    return jnp.dot(source, w_down, preferred_element_type=jnp.float32)


def shards(noise_embed, action_embed, prefix_kv, flow_step, action_mask, w_up, w_down, query_grad):
    hidden, normed_rows, target, acts = attend(noise_embed, action_embed, prefix_kv, flow_step)
    tok_rows = normed_rows.shape[0]
    mask_own = action_mask.astype(jnp.float32)[:, None]
    gathered = lax.all_gather(normed_rows, "fsdp", axis=0, tiled=True)
    pre = jnp.dot(gathered, w_up, preferred_element_type=jnp.float32)
    sig = jax.nn.sigmoid(pre)
    slopes = sig * (1.0 + pre * (1.0 - sig))
    curves = sig * (1.0 - sig) * (2.0 + pre * (1.0 - 2.0 * sig))
    active = (pre * sig).astype(jnp.bfloat16)
    output = lax.psum_scatter(
        down_rows(active, w_down).astype(jnp.bfloat16), "fsdp", scatter_dimension=0, tiled=True
    ).astype(jnp.float32)
    err = (mask_own * (hidden + output - target)).astype(jnp.bfloat16)
    err_all, mask_all = (
        lax.all_gather(err, "fsdp", axis=0, tiled=True),
        lax.all_gather(action_mask.astype(jnp.bfloat16), "fsdp", axis=0, tiled=True),
    )
    pulled = jnp.dot(err_all, w_down.T, preferred_element_type=jnp.float32)
    back = pulled * slopes
    total = tok_rows * lax.axis_size("fsdp") * lax.axis_size("dp")
    vector = query_grad
    for step in range(ITERS):
        direction_vector = jnp.dot(
            gathered, vector.astype(jnp.bfloat16), preferred_element_type=jnp.float32
        )
        linear = (slopes * direction_vector).astype(jnp.bfloat16)
        moved = lax.psum_scatter(
            down_rows(linear, w_down).astype(jnp.bfloat16), "fsdp", scatter_dimension=0, tiled=True
        ).astype(jnp.float32)
        moved_err = (mask_own * moved).astype(jnp.bfloat16)
        moved_all = lax.all_gather(moved_err, "fsdp", axis=0, tiled=True)
        second = (
            jnp.dot(moved_all, w_down.T, preferred_element_type=jnp.float32) * slopes
            + pulled * curves * direction_vector
        ).astype(jnp.bfloat16)
        partial_hv = lax.dot_general(
            gathered, second, (((0,), (0,)), ((), ())), preferred_element_type=jnp.float32
        )
        aggregate_total = lax.psum(partial_hv.astype(jnp.bfloat16), "dp").astype(jnp.float32)
        vector = query_grad + (1.0 - damping_factor) * vector - aggregate_total / total
    projected = jnp.dot(gathered, vector.astype(jnp.bfloat16), preferred_element_type=jnp.float32)
    token_terms = jnp.sum(projected * back, -1)
    demo_terms = jnp.sum(token_terms.reshape(-1, acts), -1)
    owned = lax.psum_scatter(demo_terms, "fsdp", scatter_dimension=0, tiled=True)
    return (vector, -owned / (acts * math.sqrt(D * FF)))


def solution(mesh):
    placed = (
        P(("fsdp", "dp"), None),
        P(("fsdp", "dp"), None),
        P(None, ("fsdp", "dp"), None, None),
        P(("fsdp", "dp")),
        P(("fsdp", "dp")),
        P(None, "fsdp"),
        P("fsdp", None),
        P(None, "fsdp"),
    )
    return jax.shard_map(
        shards,
        mesh=mesh,
        in_specs=placed,
        out_specs=(P(None, "fsdp"), P(("fsdp", "dp"))),
        check_vma=False,
    )
```

profile of v0, /device:TPU:0, one launch (start us, length us, event | category | flops | bytes accessed | tf_op | source)
XLA Modules:
  0.0 300.0 jit_solution(8601410605642839592)
XLA Ops:
  8.0 0.8 fusion.40
  9.1 0.8 multiply_convert_fusion.9
  9.9 1.0 fusion.21
  10.9 1.2 fusion.18
  12.1 1.1 convolution_bitcast_fusion
  13.2 0.9 multiply_reduce_fusion
  14.1 0.9 multiply_convert_fusion.8
  15.0 9.9 %all_gather.12 = bf16[64,1024]{1,0:T(8,128)(2,1)S(1)} all-gather(bf16[16,1024]{1,0:T(8,128)(2,1)S(1)} %multiply_convert_fusion.8), channel_id=1, replica_groups=mesh['fsdp'=4,'dp'=8] {'fsdp'}, dimensions={0}, use_global_device_ids=true | all-gather | bytes 163840 | tf_op jit(solution)/shard_map/all_gather | solution.py:59
  24.9 2.8 fusion.4
  28.2 1.1 convolution_convert_fusion.4
  29.5 1.1 convolution_convert_fusion.3
  30.7 23.0 %reduce-scatter.4.cloned.1.call-done = bf16[16,1024]{1,0:T(8,128)(2,1)} async-done(((bf16[64,1024]{1,0:T(8,128)(2,1)}), bf16[16,1024]{1,0:T(8,128)(2,1)}) %reduce-scatter.4.cloned.1.call-update) | async-done | bytes 32784 | tf_op jit(solution)/shard_map/reduce_scatter | solution.py:82
  53.7 27.4 %reduce-scatter.6.cloned.1.call-done = bf16[16,1024]{1,0:T(8,128)(2,1)} async-done(((bf16[64,1024]{1,0:T(8,128)(2,1)}), bf16[16,1024]{1,0:T(8,128)(2,1)}) %reduce-scatter.6.cloned.1.call-update) | async-done | bytes 32784 | tf_op jit(solution)/shard_map/reduce_scatter | solution.py:65
  81.1 0.9 fusion.38
  81.9 8.6 %all_gather.14 = bf16[64,1024]{1,0:T(8,128)(2,1)S(1)} all-gather(bf16[16,1024]{1,0:T(8,128)(2,1)S(1)} %get-tuple-element.2), channel_id=1, replica_groups=mesh['fsdp'=4,'dp'=8] {'fsdp'}, dimensions={0}, use_global_device_ids=true | all-gather | bytes 163840 | tf_op jit(solution)/shard_map/all_gather | solution.py:70
  90.5 0.8 fusion.56
  91.3 7.4 %all_gather.13 = bf16[64,1024]{1,0:T(8,128)(2,1)S(1)} all-gather(bf16[16,1024]{1,0:T(8,128)(2,1)S(1)} %get-tuple-element.3), channel_id=1, replica_groups=mesh['fsdp'=4,'dp'=8] {'fsdp'}, dimensions={0}, use_global_device_ids=true | all-gather | bytes 163840 | tf_op jit(solution)/shard_map/all_gather | solution.py:86
  98.6 2.7 convolution_convert_fusion.1
  101.3 65.1 %all-reduce.4.cloned.1.call-done = bf16[1024,1024]{1,0:T(8,128)(2,1)} async-done(((bf16[1024,1024]{1,0:T(8,128)(2,1)}), bf16[1024,1024]{1,0:T(8,128)(2,1)}) %all-reduce.4.cloned.1.call-update) | async-done | bytes 2097168 | tf_op jit(solution)/shard_map/psum | solution.py:94
  166.5 3.8 %fusion.6 = f32[64,1024]{1,0:T(8,128)S(1)} fusion(bf16[64,1024]{1,0:T(8,128)(2,1)S(1)} %all_gather.12, bf16[1024,1024]{1,0:T(8,128)(2,1)} %all-reduce.4.cloned.1.call-done, f32[1024,1024]{1,0:T(8,128)} %param.15), kind=kOutput, calls=%fused_computation.8 | convolution fusion | flops 140509184 | bytes 6684672 | tf_op jit(solution)/shard_map/dot_general | solution.py:78
  170.2 1.2 convolution_convert_fusion.2
  171.5 23.6 %reduce-scatter.8.cloned.1.call-done = bf16[16,1024]{1,0:T(8,128)(2,1)} async-done(((bf16[64,1024]{1,0:T(8,128)(2,1)}), bf16[16,1024]{1,0:T(8,128)(2,1)}) %reduce-scatter.8.cloned.1.call-update) | async-done | bytes 32784 | tf_op jit(solution)/shard_map/reduce_scatter | solution.py:82
  195.0 0.8 multiply_convert_fusion.6
  195.9 8.6 %all_gather.15 = bf16[64,1024]{1,0:T(8,128)(2,1)S(1)} all-gather(bf16[16,1024]{1,0:T(8,128)(2,1)S(1)} %multiply_convert_fusion.6), channel_id=1, replica_groups=mesh['fsdp'=4,'dp'=8] {'fsdp'}, dimensions={0}, use_global_device_ids=true | all-gather | bytes 163840 | tf_op jit(solution)/shard_map/all_gather | solution.py:86
  204.4 2.6 convolution_convert_fusion
  207.1 65.1 %all-reduce.6.cloned.1.call-done = bf16[1024,1024]{1,0:T(8,128)(2,1)} async-done(((bf16[1024,1024]{1,0:T(8,128)(2,1)}), bf16[1024,1024]{1,0:T(8,128)(2,1)}) %all-reduce.6.cloned.1.call-update) | async-done | bytes 2097168 | tf_op jit(solution)/shard_map/psum | solution.py:94
  272.2 4.9 %multiply_subtract_fusion = f32[1024,1024]{1,0:T(8,128)S(1)} fusion(bf16[1024,1024]{1,0:T(8,128)(2,1)} %all-reduce.6.cloned.1.call-done, f32[1024,1024]{1,0:T(8,128)} %param.15, bf16[1024,1024]{1,0:T(8,128)(2,1)} %all-reduce.4.cloned.1.call-done), kind=kLoop, calls=%fused_computation.2 | loop fusion | flops 10485760 | bytes 12582912 | tf_op jit(solution)/shard_map/sub | solution.py:95
  277.1 2.0 copy-done.1
  279.1 0.6 fusion.15
  280.0 0.6 dynamic-slice
  280.6 9.8 %all-reduce = f32[4]{0:T(128)S(1)} all-reduce(f32[4]{0:T(128)S(1)} %reduce_sum.59), channel_id=5, replica_groups=mesh['fsdp'=4,'dp'=8] {'fsdp'}, use_global_device_ids=true, to_apply=%region_11.0.clone | all-reduce | flops 4 | bytes 32
  290.4 1.3 dynamic-slice.1
  (35 shorter events, 1.3 us)
Async XLA Ops:
  7.2 21.1 %copy-start = (bf16[1024,1024]{1,0:T(8,128)(2,1)S(1)}, bf16[1024,1024]{1,0:T(8,128)(2,1)}, u32[]{:S(2)}) copy-start(bf16[1024,1024]{1,0:T(8,128)(2,1)} %param.14) | copy-start | bytes 6291460
  7.2 46.5 %reduce-scatter.4.cloned.1.call-start = ((), (), s32[]{:S(2)}) async-start(), calls=%async_computation.3 | async-start | bytes 163840 | tf_op jit(solution)/shard_map/reduce_scatter | solution.py:82
  24.9 2.9 copy-start.2
  29.4 1.3 copy-start.5
  29.4 51.7 %copy-start.3 = (bf16[16,1024]{1,0:T(8,128)(2,1)S(1)}, bf16[16,1024]{1,0:T(8,128)(2,1)}, u32[]{:S(2)}) copy-start(bf16[16,1024]{1,0:T(8,128)(2,1)} %param.9) | copy-start | bytes 98308
  29.4 51.7 %copy-start.4 = (bf16[16,1024]{1,0:T(8,128)(2,1)S(1)}, bf16[16,1024]{1,0:T(8,128)(2,1)}, u32[]{:S(2)}) copy-start(bf16[16,1024]{1,0:T(8,128)(2,1)} %param.8) | copy-start | bytes 98308
  29.4 51.7 %reduce-scatter.6.cloned.1.call-start = ((), (), s32[]{:S(2)}) async-start(), calls=%async_computation.4 | async-start | bytes 163840 | tf_op jit(solution)/shard_map/reduce_scatter | solution.py:65
  30.6 135.9 %all-reduce.4.cloned.1.call-start = ((), (), s32[]{:S(2)}) async-start(), calls=%async_computation.5 | async-start | bytes 4194304 | tf_op jit(solution)/shard_map/psum | solution.py:94
  101.3 93.7 %reduce-scatter.8.cloned.1.call-start = ((), (), s32[]{:S(2)}) async-start(), calls=%async_computation.6 | async-start | bytes 163840 | tf_op jit(solution)/shard_map/reduce_scatter | solution.py:82
  171.4 100.8 %all-reduce.6.cloned.1.call-start = ((), (), s32[]{:S(2)}) async-start(), calls=%async_computation.7 | async-start | bytes 4194304 | tf_op jit(solution)/shard_map/psum | solution.py:94
  277.1 2.0 copy-start.1
  279.1 0.8 copy-start.6
Sparse Core Ops, SparseCore 0:
  29.5 24.1 reduce-scatter.3
  57.2 23.8 reduce-scatter.5
  101.4 65.0 all-reduce.3
  171.6 23.4 reduce-scatter.7
  207.2 64.9 all-reduce.5
where the time goes:
time: 301 us; the launch traced here: 300 us
  waiting for transfers between devices  204 us (68%)
  blocking collectives  44.2 us (15%)
  matrix products  19.4 us (6%)
  between operations  16.5 us (5%)
  other arithmetic  11.2 us (4%)
  local copies, waits for them, and re-layouts  4.18 us (1%)
    psum x2, waiting for transfers between devices, shards(): lax.psum(partial_hv.astype(jnp.bfloat16), 'dp').astype(jnp.float32)  130 us
    reduce_scatter x2, waiting for transfers between devices, shards(): lax.psum_scatter(down_rows(linear, w_down).astype(jnp.bfloat16), 'fsdp',...  46.6 us
    reduce_scatter x1, waiting for transfers between devices, shards(): lax.psum_scatter(down_rows(active, w_down).astype(jnp.bfloat16), 'fsdp',...  27.4 us
    all_gather x2, blocking collectives, shards(): moved_all = lax.all_gather(moved_err, 'fsdp', axis=0, tiled=True)  15.9 us
    all_gather x1, blocking collectives, shards(): gathered = lax.all_gather(normed_rows, 'fsdp', axis=0, tiled=True)  9.91 us
    unnamed x1, blocking collectives  9.81 us
    all_gather x1, blocking collectives, shards(): lax.all_gather(err, 'fsdp', axis=0, tiled=True)  8.56 us
    dot_general x3, matrix products, shards(): jnp.dot(gathered, vector.astype(jnp.bfloat16), preferred_element_type=jnp...  7.2 us
  transfers between devices with their start and end apart: 5, of which 5 were waited for; matrix products, arithmetic and copies ran while one was open for 0% of the time, Pallas kernels for 0%

commit v1 on v0

v1 whole, which is shorter than its diff:
```python
import math

import jax
import jax.numpy as jnp
from jax import lax
from jax.sharding import PartitionSpec as P

STEPS_T = 10

epsilon = 1e-06
sharpness_divisor = 6.0
keep = 1.0 - 0.01


def attend(noise_embed, action_embed, prefix_kv, flow_step):
    demos = flow_step.shape[0]
    acts = noise_embed.shape[0] // demos
    channel_span = prefix_kv.shape[3]
    width = noise_embed.shape[1]
    times = (flow_step.astype(jnp.float32) + 1.0) / (STEPS_T + 1.0)
    per_token = jnp.repeat(times, acts)[:, None]
    noisy = noise_embed.astype(jnp.float32)
    clean = action_embed.astype(jnp.float32)
    inputs = per_token * noisy + (1.0 - per_token) * clean
    target = noisy - clean
    queries = inputs.reshape(demos, acts, width // channel_span, channel_span)
    probe_length = (
        queries * lax.rsqrt(jnp.mean(queries * queries, -1, keepdims=True) + epsilon)
    ).astype(jnp.bfloat16)
    keys = prefix_kv[0].astype(jnp.float32)
    lookup_length = (keys * lax.rsqrt(jnp.mean(keys * keys, -1, keepdims=True) + epsilon)).astype(
        jnp.bfloat16
    )
    match_energies = jnp.einsum(
        "zilf,zgf->zilg", probe_length, lookup_length, preferred_element_type=jnp.float32
    ) * (sharpness_divisor / channel_span)
    expo = jnp.exp(match_energies)
    weights = (expo / jnp.sum(expo, -1, keepdims=True)).astype(jnp.bfloat16)
    mixed = jnp.einsum("dahp,dpe->dahe", weights, prefix_kv[1], preferred_element_type=jnp.float32)
    hidden = inputs + mixed.reshape(demos * acts, width)
    normed_rows = (
        hidden * lax.rsqrt(jnp.mean(hidden * hidden, -1, keepdims=True) + epsilon)
    ).astype(jnp.bfloat16)
    return (hidden, normed_rows, target, acts)


def dot32(a, b):
    return jnp.dot(a, b, preferred_element_type=jnp.float32)


def shards(noise_embed, action_embed, prefix_kv, flow_step, action_mask, w_up, w_down, query_grad):
    hidden, normed_rows, target, acts = attend(noise_embed, action_embed, prefix_kv, flow_step)
    tok_rows, width = normed_rows.shape
    nf = lax.axis_size("fsdp")
    mask_own = action_mask.astype(jnp.float32)[:, None]
    gathered = lax.all_gather(normed_rows, "fsdp", axis=0, tiled=True)
    every = lax.all_gather(gathered, "dp", axis=0, tiled=True)
    rows = gathered.shape[0]
    total = tok_rows * nf * lax.axis_size("dp")
    pre = dot32(gathered, w_up)
    sig = jax.nn.sigmoid(pre)
    slopes = sig * (1.0 + pre * (1.0 - sig))
    curves = sig * (1.0 - sig) * (2.0 + pre * (1.0 - 2.0 * sig))
    active = (pre * sig).astype(jnp.bfloat16)
    tangent0 = dot32(gathered, query_grad.astype(jnp.bfloat16))
    linear = (slopes * tangent0).astype(jnp.bfloat16)
    both = jnp.concatenate(
        [dot32(active, w_down).astype(jnp.bfloat16), dot32(linear, w_down).astype(jnp.bfloat16)], 1
    )
    both = lax.psum_scatter(both, "fsdp", scatter_dimension=0, tiled=True).astype(jnp.float32)
    err = mask_own * (hidden + both[:, :width] - target)
    moved_err = mask_own * both[:, width:]
    pair = jnp.concatenate([err, moved_err], 1).astype(jnp.bfloat16)
    pair = lax.all_gather(pair, "fsdp", axis=0, tiled=True)
    pulled = dot32(pair[:, :width], w_down.T)
    back = pulled * slopes
    bent = pulled * curves
    second = (dot32(pair[:, width:], w_down.T) * slopes + bent * tangent0).astype(jnp.bfloat16)
    seconds0 = lax.all_gather(second, "dp", axis=0, tiled=True)
    gram = (lax.dot_general(gathered, every, (((1,), (1,)), ((), ())), preferred_element_type=jnp.float32) / total).astype(jnp.bfloat16)
    tangent1 = (1.0 + keep) * tangent0 - dot32(gram, seconds0)
    linear = (slopes * tangent1).astype(jnp.bfloat16)
    moved = lax.psum_scatter(
        dot32(linear, w_down).astype(jnp.bfloat16), "fsdp", scatter_dimension=0, tiled=True
    ).astype(jnp.float32)
    moved_all = lax.all_gather((mask_own * moved).astype(jnp.bfloat16), "fsdp", axis=0, tiled=True)
    second = (dot32(moved_all, w_down.T) * slopes + bent * tangent1).astype(jnp.bfloat16)
    seconds1 = lax.all_gather(second, "dp", axis=0, tiled=True)
    mix = (keep * seconds0.astype(jnp.float32) + seconds1.astype(jnp.float32)).astype(jnp.bfloat16)
    change = lax.dot_general(every, mix, (((0,), (0,)), ((), ())), preferred_element_type=jnp.float32) / total
    scale = 1.0 + keep + keep * keep
    vector = scale * query_grad - change
    projected = scale * tangent0 - dot32(gram, mix)
    token_terms = jnp.sum(projected * back, -1)
    demo_terms = jnp.sum(token_terms.reshape(-1, acts), -1)
    owned = lax.psum_scatter(demo_terms, "fsdp", scatter_dimension=0, tiled=True)
    return (vector, -owned / (acts * math.sqrt(query_grad.shape[0] * query_grad.shape[1] * nf)))


def solution(mesh):
    placed = (
        P(("fsdp", "dp"), None),
        P(("fsdp", "dp"), None),
        P(None, ("fsdp", "dp"), None, None),
        P(("fsdp", "dp")),
        P(("fsdp", "dp")),
        P(None, "fsdp"),
        P("fsdp", None),
        P(None, "fsdp"),
    )
    return jax.shard_map(
        shards,
        mesh=mesh,
        in_specs=placed,
        out_specs=(P(None, "fsdp"), P(("fsdp", "dp"))),
        check_vma=False,
    )
```

time: 301 us -> 181 us (0.60)
  waiting for transfers between devices: 204 us -> 90.4 us
  blocking collectives: 44.2 us -> 37.2 us
  matrix products: 19.4 us -> 24.6 us
  other arithmetic: 11.2 us -> 7.1 us
    psum x2 -> x0, waiting for transfers between devices: 130 us -> none  [shards(): lax.psum(partial_hv.astype(jnp.bfloat16), 'dp').astype(jnp.float32)]
    all_gather x0 -> x3, waiting for transfers between devices: none -> 42.4 us  [the longest x1 22.1 us: shards(): seconds1 = lax.all_gather(second, 'dp', axis=0, tiled=True)]
    reduce_scatter x3 -> x2, waiting for transfers between devices: 73.9 us -> 47.5 us  [the longest x1 23.9 us: shards(): lax.psum_scatter(both, 'fsdp', scatter_dimension=0, tiled=True)]
    all_gather x3 -> x2, blocking collectives: 24.5 us -> 17.5 us  [the longest x1 8.96 us: shards(): pair = lax.all_gather(pair, 'fsdp', axis=0, tiled=True)]
    dot_general x10 -> x12, matrix products: 17.2 us -> 22.3 us  [the longest x10 14.4 us: dot32(): return jnp.dot(a, b, preferred_element_type=jnp.float32)]
    sub x1 -> x0, other arithmetic: 4.88 us -> none  [shards(): query_grad + (1.0 - damping_factor) * vector - aggregate_total / total]
  transfers between devices with their start and end apart: 5 -> 5, of which waited for: 5 -> 4; matrix products, arithmetic and copies ran while one was open for 0% -> 3% of each run, Pallas kernels for 0% -> 0%
where the time goes in v1:
time: 181 us; the launch traced here: 180 us
  waiting for transfers between devices  90.4 us (50%)
  blocking collectives  37.2 us (21%)
  matrix products  24.6 us (14%)
  between operations  18.5 us (10%)
  other arithmetic  7.1 us (4%)
  local copies, waits for them, and re-layouts  2.09 us (1%)
    reduce_scatter x1, waiting for transfers between devices, shards(): lax.psum_scatter(both, 'fsdp', scatter_dimension=0, tiled=True)  23.9 us
    reduce_scatter x1, waiting for transfers between devices, shards(): lax.psum_scatter(dot32(linear, w_down).astype(jnp.bfloat16), 'fsdp', scat...  23.6 us
    all_gather x1, waiting for transfers between devices, shards(): seconds1 = lax.all_gather(second, 'dp', axis=0, tiled=True)  22.1 us
    all_gather x1, waiting for transfers between devices, shards(): seconds0 = lax.all_gather(second, 'dp', axis=0, tiled=True)  20.3 us
    dot_general x10, matrix products, dot32(): return jnp.dot(a, b, preferred_element_type=jnp.float32)  14.4 us
    all_gather x1, blocking collectives, shards(): gathered = lax.all_gather(normed_rows, 'fsdp', axis=0, tiled=True)  9.91 us
    unnamed x1, blocking collectives  9.8 us
    all_gather x1, blocking collectives, shards(): pair = lax.all_gather(pair, 'fsdp', axis=0, tiled=True)  8.96 us
  transfers between devices with their start and end apart: 5, of which 4 were waited for; matrix products, arithmetic and copies ran while one was open for 3% of the time, Pallas kernels for 0%

profile of v1, /device:TPU:0, one launch (start us, length us, event | category | flops | bytes accessed | tf_op | source)
XLA Modules:
  0.0 180.1 jit_solution(14916627800263029740)
XLA Ops:
  8.8 1.0 fusion.12
  9.9 0.8 fusion.33
  10.9 0.8 multiply_convert_fusion.8
  11.7 1.2 fusion.9
  12.9 1.1 convolution_bitcast_fusion
  14.0 0.9 multiply_reduce_fusion
  15.0 0.9 multiply_convert_fusion.7
  15.8 9.9 %all_gather.18 = bf16[64,1024]{1,0:T(8,128)(2,1)S(1)} all-gather(bf16[16,1024]{1,0:T(8,128)(2,1)S(1)} %multiply_convert_fusion.7), channel_id=1, replica_groups=mesh['fsdp'=4,'dp'=8] {'fsdp'}, dimensions={0}, use_global_device_ids=true | all-gather | bytes 163840 | tf_op jit(solution)/shard_map/all_gather | solution.py:56
  25.7 2.1 %fusion.44 = f32[64,1024]{1,0:T(8,128)S(1)} fusion(bf16[64,1024]{1,0:T(8,128)(2,1)S(1)} %all_gather.18, bf16[1024,1024]{1,0:T(8,128)(2,1)} %param.13), kind=kOutput, calls=%fused_computation.75 | convolution fusion | flops 134217728 | bytes 2490368 | tf_op jit(solution)/shard_map/dot_general | solution.py:48
  27.9 2.8 %fusion = f32[64,1024]{1,0:T(8,128)S(1)} fusion(bf16[64,1024]{1,0:T(8,128)(2,1)S(1)} %all_gather.18, f32[1024,1024]{1,0:T(8,128)} %param.15), kind=kOutput, calls=%fused_computation.2 | convolution fusion | flops 135266304 | bytes 4587520 | tf_op jit(solution)/shard_map/dot_general | solution.py:48
  31.2 0.5 convolution_convert_fusion.1
  31.7 0.7 pad_maximum_fusion
  32.5 0.5 all-gather.4.cloned.1.call-update
  33.0 23.9 %reduce-scatter.3.cloned.1.call-done = bf16[16,2048]{1,0:T(8,128)(2,1)} async-done(((bf16[64,2048]{1,0:T(8,128)(2,1)}), bf16[16,2048]{1,0:T(8,128)(2,1)}) %reduce-scatter.3.cloned.1.call-update) | async-done | bytes 65552 | tf_op jit(solution)/shard_map/reduce_scatter | solution.py:70
  57.0 0.8 convert_element_type.148
  57.9 9.0 %all_gather.20 = bf16[64,2048]{1,0:T(8,128)(2,1)S(1)} all-gather(bf16[16,2048]{1,0:T(8,128)(2,1)S(1)} %pad_maximum_fusion.1), channel_id=1, replica_groups=mesh['fsdp'=4,'dp'=8] {'fsdp'}, dimensions={0}, use_global_device_ids=true | all-gather | bytes 327680 | tf_op jit(solution)/shard_map/all_gather | solution.py:74
  66.9 0.8 fusion.19
  67.7 1.4 fusion.5
  69.2 1.7 fusion.8
  70.9 20.3 %all-gather.6.cloned.1.call-done = bf16[512,1024]{1,0:T(8,128)(2,1)} async-done(((bf16[64,1024]{1,0:T(8,128)(2,1)}), bf16[512,1024]{1,0:T(8,128)(2,1)}) %all-gather.6.cloned.1.call-update) | async-done | bytes 1048592 | tf_op jit(solution)/shard_map/all_gather | solution.py:79
  91.2 1.5 convolution_subtract_fusion.1
  92.7 1.1 convolution_convert_fusion
  93.9 23.6 %reduce-scatter.5.cloned.1.call-done = bf16[16,1024]{1,0:T(8,128)(2,1)} async-done(((bf16[64,1024]{1,0:T(8,128)(2,1)}), bf16[16,1024]{1,0:T(8,128)(2,1)}) %reduce-scatter.5.cloned.1.call-update) | async-done | bytes 32784 | tf_op jit(solution)/shard_map/reduce_scatter | solution.py:83
  117.5 0.8 multiply_convert_fusion.6
  118.3 8.6 %all_gather.22 = bf16[64,1024]{1,0:T(8,128)(2,1)S(1)} all-gather(bf16[16,1024]{1,0:T(8,128)(2,1)S(1)} %multiply_convert_fusion.6), channel_id=1, replica_groups=mesh['fsdp'=4,'dp'=8] {'fsdp'}, dimensions={0}, use_global_device_ids=true | all-gather | bytes 163840 | tf_op jit(solution)/shard_map/all_gather | solution.py:86
  126.9 1.4 fusion.6
  128.4 22.1 %all-gather.8.cloned.1.call-done = bf16[512,1024]{1,0:T(8,128)(2,1)} async-done(((bf16[64,1024]{1,0:T(8,128)(2,1)}), bf16[512,1024]{1,0:T(8,128)(2,1)}) %all-gather.8.cloned.1.call-update) | async-done | bytes 1048592 | tf_op jit(solution)/shard_map/all_gather | solution.py:88
  150.4 2.2 %fusion.7 = f32[64]{0:T(128)S(1)} fusion(bf16[64,512]{1,0:T(8,128)(2,1)S(1)} %fusion.8, bf16[512,1024]{1,0:T(8,128)(2,1)} %all-gather.8.cloned.1.call-done, bf16[512,1024]{1,0:T(8,128)(2,1)} %all-gather.6.cloned.1.call-done, f32[64,1024]{1,0:T(8,128)} %copy-done.7, f32[64,1024]{1,0:T(8,128)S(1)} %fusion, f32[64,1024]{1,0:T(8,128)} %copy-done.6), kind=kOutput, calls=%fused_computation.16 | convolution fusion | flops 70516672 | bytes 2949376 | tf_op jit(solution)/shard_map/dot_general | solution.py:48
  152.9 0.6 dynamic-slice
  153.5 9.8 %all-reduce = f32[4]{0:T(128)S(1)} all-reduce(f32[4]{0:T(128)S(1)} %reduce_sum.59), channel_id=4, replica_groups=mesh['fsdp'=4,'dp'=8] {'fsdp'}, use_global_device_ids=true, to_apply=%region_8.0.clone | all-reduce | flops 4 | bytes 32
  163.3 1.2 dynamic-slice.1
  165.2 6.2 %multiply_subtract_fusion = f32[1024,1024]{1,0:T(8,128)} fusion(f32[1024,1024]{1,0:T(8,128)} %param.15, bf16[512,1024]{1,0:T(8,128)(2,1)S(1)} %copy-done.1, bf16[512,1024]{1,0:T(8,128)(2,1)} %all-gather.8.cloned.1.call-done, bf16[512,1024]{1,0:T(8,128)(2,1)} %all-gather.6.cloned.1.call-done), kind=kOutput, calls=%fused_computation | convolution fusion | flops 1079508992 | bytes 11534336 | tf_op jit(solution)/shard_map/dot_general | solution.py:90
  (44 shorter events, 1.4 us)
Async XLA Ops:
  8.0 22.6 %copy-start = (bf16[1024,1024]{1,0:T(8,128)(2,1)S(1)}, bf16[1024,1024]{1,0:T(8,128)(2,1)}, u32[]{:S(2)}) copy-start(bf16[1024,1024]{1,0:T(8,128)(2,1)} %param.14) | copy-start | bytes 6291460
  8.0 48.9 %reduce-scatter.3.cloned.1.call-start = ((), (), s32[]{:S(2)}) async-start(), calls=%async_computation.3 | async-start | bytes 327680 | tf_op jit(solution)/shard_map/reduce_scatter | solution.py:70
  25.7 4.9 %copy-start.2 = (bf16[64,1024]{1,0:T(8,128)(2,1)}, bf16[64,1024]{1,0:T(8,128)(2,1)S(1)}, u32[]{:S(2)}) copy-start(bf16[64,1024]{1,0:T(8,128)(2,1)S(1)} %all_gather.18) | copy-start | bytes 393220
  27.9 99.0 %copy-start.6 = (f32[64,1024]{1,0:T(8,128)}, f32[64,1024]{1,0:T(8,128)S(1)}, u32[]{:S(2)}) copy-start(f32[64,1024]{1,0:T(8,128)S(1)} %fusion.44) | copy-start | bytes 786436
  31.1 1.9 %copy-start.8 = (s32[16]{0:T(128)S(1)}, s32[16]{0:T(128)}, u32[]{:S(2)}) copy-start(s32[16]{0:T(128)} %param.12) | copy-start | bytes 196
  31.1 26.7 %copy-start.4 = (bf16[16,1024]{1,0:T(8,128)(2,1)S(1)}, bf16[16,1024]{1,0:T(8,128)(2,1)}, u32[]{:S(2)}) copy-start(bf16[16,1024]{1,0:T(8,128)(2,1)} %param.9) | copy-start | bytes 98308
  31.1 26.7 %copy-start.5 = (bf16[16,1024]{1,0:T(8,128)(2,1)S(1)}, bf16[16,1024]{1,0:T(8,128)(2,1)}, u32[]{:S(2)}) copy-start(bf16[16,1024]{1,0:T(8,128)(2,1)} %param.8) | copy-start | bytes 98308
  32.4 36.8 %all-gather.4.cloned.1.call-start = ((), (), s32[]{:S(2)}) async-start(), calls=%async_computation.2 | async-start | bytes 1179648 | tf_op jit(solution)/shard_map/all_gather | solution.py:57
  33.0 58.2 %all-gather.6.cloned.1.call-start = ((), (), s32[]{:S(2)}) async-start(), calls=%async_computation.4 | async-start | bytes 1179648 | tf_op jit(solution)/shard_map/all_gather | solution.py:79
  67.6 59.2 %copy-start.7 = (f32[64,1024]{1,0:T(8,128)}, f32[64,1024]{1,0:T(8,128)S(1)}, u32[]{:S(2)}) copy-start(f32[64,1024]{1,0:T(8,128)S(1)} %fusion.19) | copy-start | bytes 786436
  67.7 1.5 copy-start.3
  69.1 48.4 %reduce-scatter.5.cloned.1.call-start = ((), (), s32[]{:S(2)}) async-start(), calls=%async_computation.5 | async-start | bytes 163840 | tf_op jit(solution)/shard_map/reduce_scatter | solution.py:83
  93.9 56.5 %all-gather.8.cloned.1.call-start = ((), (), s32[]{:S(2)}) async-start(), calls=%async_computation.6 | async-start | bytes 1179648 | tf_op jit(solution)/shard_map/all_gather | solution.py:88
  128.3 24.6 %copy-start.9 = (u32[32]{0:T(128)S(1)}, u32[32]{0:T(128)}, u32[]{:S(2)}) copy-start(u32[32]{0:T(128)} %constant.48) | copy-start | bytes 388
  128.3 36.8 %copy-start.1 = (bf16[512,1024]{1,0:T(8,128)(2,1)S(1)}, bf16[512,1024]{1,0:T(8,128)(2,1)}, u32[]{:S(2)}) copy-start(bf16[512,1024]{1,0:T(8,128)(2,1)} %all-gather.4.cloned.1.call-done) | copy-start | bytes 3145732
Sparse Core Ops, SparseCore 0:
  32.5 24.3 reduce-scatter.2
  94.0 23.4 reduce-scatter.4
Sparse Core Ops, SparseCore 1:
  34.5 22.2 all-gather.3
  69.2 21.9 all-gather.5
  128.4 21.9 all-gather.7

commit v2 on v1

v2 whole, which is shorter than its diff:
```python
import functools
import math

import jax
import jax.numpy as jnp
from jax import lax
from jax.experimental import pallas as pl
from jax.experimental.pallas import tpu as pltpu
from jax.sharding import PartitionSpec as P

STEPS_T = 10
CORES = 2

epsilon = 1e-06
sharpness_divisor = 6.0
keep = 1.0 - 0.01

BF = jnp.bfloat16
F32 = jnp.float32
MESH = pl.DeviceIdType.MESH


def dot32(a, b):
    return jnp.dot(a, b, preferred_element_type=F32)


def dot_t(a, b):
    return lax.dot_general(a, b, (((1,), (1,)), ((), ())), preferred_element_type=F32)


def loop(count, body):
    if count == 1:
        body(0)
    else:
        pl.loop(0, count)(body)


def tile(i, size):
    return pl.ds(pl.multiple_of(i * size, size), size)


def attend(noise, action, kv, flow):
    acts, width = noise.shape
    span = kv.shape[3]
    heads = width // span
    time = (flow[0].astype(F32) + 1.0) / (STEPS_T + 1.0)
    noisy = noise[...].astype(F32)
    clean = action[...].astype(F32)
    inputs = time * noisy + (1.0 - time) * clean
    queries = jnp.concatenate([inputs[:, h * span : (h + 1) * span] for h in range(heads)], 0)
    queries = queries * lax.rsqrt(jnp.mean(queries * queries, -1, keepdims=True) + epsilon)
    keys = kv[0, 0].astype(F32)
    keys = keys * lax.rsqrt(jnp.mean(keys * keys, -1, keepdims=True) + epsilon)
    expo = jnp.exp(dot_t(queries.astype(BF), keys.astype(BF)) * (sharpness_divisor / span))
    weights = (expo / jnp.sum(expo, -1, keepdims=True)).astype(BF)
    mixed = dot32(weights, kv[1, 0])
    mixed = jnp.concatenate([mixed[h * acts : (h + 1) * acts] for h in range(heads)], 1)
    hidden = inputs + mixed
    normed = hidden * lax.rsqrt(jnp.mean(hidden * hidden, -1, keepdims=True) + epsilon)
    return normed.astype(BF), hidden - (noisy - clean)


def kernel(
    nf, nd,
    noise, action, kv, flow, mask, w_up_h, w_down_h, grad_h,
    every_o, mix_o, score,
    w_up, w_down, grad, every, seconds0, seconds1, gram,
    slopes, curves, pulled, tan0, tan1, lhs, part, land0, land1, pair0, pair1,
    resid, tally, tally_in,
    load_sem, store_sem, f_send, f_recv, z_send, z_recv, c_send, c_recv,
):
    acts, width = noise.shape
    hid = w_up.shape[1]
    rows = nf * acts
    total = nd * rows
    chips = nd // CORES
    f = lax.axis_index("fsdp")
    d = lax.axis_index("dp")
    chip, core = d // CORES, d % CORES
    sibling = chip * CORES + (1 - core)

    def f_peer(k):
        return lax.rem(f + k, nf)

    def d_peer(k):
        return lax.rem(chip + k, chips) * CORES + core

    def d_from(k):
        return lax.rem(chip + chips - k, chips) * CORES + core

    barrier = pltpu.get_barrier_semaphore()
    for k in range(1, nf):
        pl.semaphore_signal(barrier, inc=1, device_id=(f_peer(k), d), device_id_type=MESH)
    for k in range(1, chips):
        pl.semaphore_signal(barrier, inc=1, device_id=(f, d_peer(k)), device_id_type=MESH)
    pl.semaphore_signal(barrier, inc=1, device_id=(f, sibling), device_id_type=MESH)

    loads = [
        pltpu.make_async_copy(src, dst, load_sem.at[i])
        for i, (src, dst) in enumerate(((w_up_h, w_up), (grad_h, grad), (w_down_h, w_down)))
    ]
    for load in loads:
        load.start()

    def remote(src, dst, send, recv, who):
        copy = pltpu.make_async_remote_copy(
            src_ref=src, dst_ref=dst, send_sem=send, recv_sem=recv, device_id=who, device_id_type=MESH
        )
        copy.start()
        return copy

    sent = []

    def fsdp(phase, src, dst):
        copies = [
            remote(src(f_peer(k)), dst(k), f_send.at[phase, k], f_recv.at[phase, k], (f_peer(k), d))
            for k in range(1, nf)
        ]
        if phase not in (1, 2):
            sent.extend(copies)
        return copies

    def landed(copies):
        for copy in copies:
            copy.wait_recv()

    def dp_start(phase, buf):
        mine = buf.at[tile(d, rows), :]
        z = [
            remote(mine, mine, z_send.at[phase, k], z_recv.at[phase, k], (f, d_peer(k)))
            for k in range(1, chips)
        ]
        c = [remote(mine, mine, c_send.at[phase, 0], c_recv.at[phase, 0], (f, sibling))]
        sent.extend(z)
        sent.extend(c)
        return z, c

    def dp_forward(phase, buf, z, c):
        for k in range(1, chips):
            z[k - 1].wait_recv()
            block = buf.at[tile(d_from(k), rows), :]
            copy = remote(block, block, c_send.at[phase, k], c_recv.at[phase, k], (f, sibling))
            sent.append(copy)
            c.append(copy)

    normed, left = attend(noise, action, kv, flow)
    resid[...] = left
    own = pl.ds(pl.multiple_of(d * rows + f * acts, acts), acts)
    every[own, :] = normed
    lane = lax.broadcasted_iota(jnp.int32, (acts, acts), 1)
    line = lax.broadcasted_iota(jnp.int32, (acts, acts), 0)
    valid = jnp.sum(
        jnp.where(lane == line, jnp.broadcast_to(mask[...].astype(F32), (acts, acts)), 0.0), -1, keepdims=True
    )
    pl.semaphore_wait(barrier, nf - 1 + chips)

    mine = every.at[own, :]
    landed(fsdp(0, lambda p: mine, lambda k: mine))
    group_at = tile(d, rows)
    z_n, c_n = dp_start(0, every)

    loads[0].wait()
    loads[1].wait()
    step = min(256, hid)

    def first(i):
        cut = tile(i, step)
        group = every[group_at, :]
        pre = dot32(group, w_up[:, cut])
        tangent = dot32(group, grad[:, cut].astype(BF))
        sig = 1.0 / (1.0 + jnp.exp(-pre))
        slope = sig * (1.0 + pre * (1.0 - sig))
        slopes[:, cut] = slope
        curves[:, cut] = sig * (1.0 - sig) * (2.0 + pre * (1.0 - 2.0 * sig))
        tan0[:, cut] = tangent
        lhs[0:rows, cut] = (pre * sig).astype(BF)
        lhs[rows : 2 * rows, cut] = (slope * tangent).astype(BF)

    loop(hid // step, first)
    loads[2].wait()
    wide = min(256, width)

    def down(i):
        cut = tile(i, wide)
        part[:, cut] = dot32(lhs[...], w_down[:, cut]).astype(BF)

    loop(width // wide, down)

    def rows_of(p, q):
        return pl.ds(pl.multiple_of(q * rows + p * acts, acts), acts)

    outs = fsdp(1, lambda p: part.at[rows_of(p, 0), :], lambda k: land0.at[k, 0:acts, :])
    moves = fsdp(2, lambda p: part.at[rows_of(p, 1), :], lambda k: land0.at[k, acts : 2 * acts, :])

    def summed(copies, q, land, lo):
        value = part[rows_of(f, q), :].astype(F32)
        for k in range(1, nf):
            copies[k - 1].wait_recv()
            value = value + land[k, lo : lo + acts, :].astype(F32)
        return value

    err = (valid * (resid[...] + summed(outs, 0, land0, 0))).astype(BF)
    pair0[rows_of(f, 0), :] = err
    errs = fsdp(3, lambda p: pair0.at[rows_of(f, 0), :], lambda k: pair0.at[rows_of(f, 0), :])
    pair0[rows_of(f, 1), :] = (valid * summed(moves, 1, land0, acts)).astype(BF)
    merrs = fsdp(4, lambda p: pair0.at[rows_of(f, 1), :], lambda k: pair0.at[rows_of(f, 1), :])
    dp_forward(0, every, z_n, c_n)
    landed(errs)
    landed(merrs)

    def bend(i):
        cut = tile(i, step)
        both = dot_t(pair0[...], w_down[cut, :])
        pull = both[0:rows]
        pulled[:, cut] = pull
        seconds0[group_at, cut] = (
            both[rows : 2 * rows] * slopes[:, cut] + pull * curves[:, cut] * tan0[:, cut]
        ).astype(BF)

    loop(hid // step, bend)
    z_0, c_0 = dp_start(1, seconds0)
    landed(c_n)
    keep_every = pltpu.make_async_copy(every, every_o, store_sem.at[0])
    keep_every.start()
    chunk = min(512, total)

    def grams(i):
        cut = tile(i, chunk)
        gram[:, cut] = (dot_t(every[group_at, :], every[cut, :]) / total).astype(BF)

    loop(total // chunk, grams)
    dp_forward(1, seconds0, z_0, c_0)
    landed(c_0)

    def fold(seconds, cut):
        if total == chunk:
            return dot32(gram[...], seconds[:, cut])
        return lax.fori_loop(
            0,
            total // chunk,
            lambda j, v: v + dot32(gram[:, tile(j, chunk)], seconds[tile(j, chunk), cut]),
            jnp.zeros((rows, step), F32),
        )

    def again(i):
        cut = tile(i, step)
        tangent = (1.0 + keep) * tan0[:, cut] - fold(seconds0, cut)
        tan1[:, cut] = tangent
        lhs[0:rows, cut] = (slopes[:, cut] * tangent).astype(BF)

    loop(hid // step, again)
    for copy in outs + moves:
        copy.wait_send()

    def down_again(i):
        cut = tile(i, wide)
        part[0:rows, cut] = dot32(lhs[0:rows, :], w_down[:, cut]).astype(BF)

    loop(width // wide, down_again)
    moves1 = fsdp(5, lambda p: part.at[rows_of(p, 0), :], lambda k: land1.at[k])
    pair1[rows_of(f, 0), :] = (valid * summed(moves1, 0, land1, 0)).astype(BF)
    landed(fsdp(6, lambda p: pair1.at[rows_of(f, 0), :], lambda k: pair1.at[rows_of(f, 0), :]))

    def bend_again(i):
        cut = tile(i, step)
        both = dot_t(pair1[...], w_down[cut, :])
        seconds1[group_at, cut] = (
            both * slopes[:, cut] + pulled[:, cut] * curves[:, cut] * tan1[:, cut]
        ).astype(BF)

    loop(hid // step, bend_again)
    z_1, c_1 = dp_start(2, seconds1)
    dp_forward(2, seconds1, z_1, c_1)
    landed(c_1)
    for copy in sent:
        copy.wait_send()

    def blend(i):
        cut = tile(i, rows)
        seconds1[cut, :] = (
            keep * seconds0[cut, :].astype(F32) + seconds1[cut, :].astype(F32)
        ).astype(BF)

    loop(nd, blend)
    keep_mix = pltpu.make_async_copy(seconds1, mix_o, store_sem.at[1])
    keep_mix.start()
    scale = 1.0 + keep + keep * keep

    def rate(i, terms):
        cut = tile(i, step)
        projected = scale * tan0[:, cut] - fold(seconds1, cut)
        return terms + projected * (pulled[:, cut] * slopes[:, cut])

    terms = lax.fori_loop(0, hid // step, rate, jnp.zeros((rows, step), F32))
    for p in range(nf):
        one = jnp.sum(terms[p * acts : (p + 1) * acts], 0, keepdims=True)
        tally[p] = jnp.broadcast_to(jnp.sum(one, -1, keepdims=True), tally.shape[1:])
    votes = [
        remote(tally.at[f_peer(k)], tally_in.at[k], f_send.at[7, k], f_recv.at[7, k], (f_peer(k), d))
        for k in range(1, nf)
    ]
    value = tally[f]
    for k in range(1, nf):
        votes[k - 1].wait_recv()
        value = value + tally_in[k]
    score[...] = -value / (acts * math.sqrt(width * hid * nf))
    for copy in votes:
        copy.wait_send()
    keep_every.wait()
    keep_mix.wait()


def finish(total, every, mix, grad, out):
    change = lax.dot_general(
        every[...], mix[...], (((0,), (0,)), ((), ())), preferred_element_type=F32
    )
    out[...] = (1.0 + keep + keep * keep) * grad[...] - change / total


def shards(nf, nd, noise, action, kv, flow, mask, w_up, w_down, grad):
    acts, width = noise.shape
    hid = w_up.shape[1]
    rows = nf * acts
    total = nd * rows
    vmem = pl.BlockSpec(memory_space=pltpu.VMEM)
    anywhere = pl.BlockSpec(memory_space=pl.ANY)
    dma = pltpu.SemaphoreType.DMA
    chips = nd // CORES
    every, mix, score = pl.pallas_call(
        functools.partial(kernel, nf, nd),
        out_shape=(
            jax.ShapeDtypeStruct((total, width), BF),
            jax.ShapeDtypeStruct((total, hid), BF),
            jax.ShapeDtypeStruct((8, 128), F32),
        ),
        in_specs=[
            vmem, vmem, vmem, pl.BlockSpec(memory_space=pltpu.SMEM), vmem, anywhere, anywhere, anywhere,
        ],
        out_specs=(anywhere, anywhere, vmem),
        scratch_shapes=[
            pltpu.VMEM((width, hid), BF),
            pltpu.VMEM((hid, width), BF),
            pltpu.VMEM((width, hid), F32),
            pltpu.VMEM((total, width), BF),
            pltpu.VMEM((total, hid), BF),
            pltpu.VMEM((total, hid), BF),
            pltpu.VMEM((rows, total), BF),
            pltpu.VMEM((rows, hid), F32),
            pltpu.VMEM((rows, hid), F32),
            pltpu.VMEM((rows, hid), F32),
            pltpu.VMEM((rows, hid), F32),
            pltpu.VMEM((rows, hid), F32),
            pltpu.VMEM((2 * rows, hid), BF),
            pltpu.VMEM((2 * rows, width), BF),
            pltpu.VMEM((nf, 2 * acts, width), BF),
            pltpu.VMEM((nf, acts, width), BF),
            pltpu.VMEM((2 * rows, width), BF),
            pltpu.VMEM((rows, width), BF),
            pltpu.VMEM((acts, width), F32),
            pltpu.VMEM((nf, 8, 128), F32),
            pltpu.VMEM((nf, 8, 128), F32),
            dma((3,)),
            dma((2,)),
            dma((8, nf)),
            dma((8, nf)),
            dma((3, chips)),
            dma((3, chips)),
            dma((3, chips)),
            dma((3, chips)),
        ],
        compiler_params=pltpu.CompilerParams(
            collective_id=0, has_side_effects=True, vmem_limit_bytes=52 * 1024 * 1024
        ),
        name="lissa",
    )(noise, action, kv, flow, mask.reshape(1, acts), w_up, w_down, grad)
    strip = 128
    vector = pl.pallas_call(
        functools.partial(finish, total),
        out_shape=jax.ShapeDtypeStruct((width, hid), F32),
        grid=(width // strip,),
        in_specs=[
            pl.BlockSpec((total, strip), lambda i: (0, i)),
            pl.BlockSpec((total, hid), lambda i: (0, 0)),
            pl.BlockSpec((strip, hid), lambda i: (i, 0)),
        ],
        out_specs=pl.BlockSpec((strip, hid), lambda i: (i, 0)),
        compiler_params=pltpu.CompilerParams(vmem_limit_bytes=40 * 1024 * 1024),
        name="finish",
    )(every, mix, grad)
    return vector, score[0, 0:1]


def solution(mesh):
    placed = (
        P(("fsdp", "dp"), None),
        P(("fsdp", "dp"), None),
        P(None, ("fsdp", "dp"), None, None),
        P(("fsdp", "dp")),
        P(("fsdp", "dp")),
        P(None, "fsdp"),
        P("fsdp", None),
        P(None, "fsdp"),
    )
    return jax.shard_map(
        functools.partial(shards, mesh.shape["fsdp"], mesh.shape["dp"]),
        mesh=mesh,
        in_specs=placed,
        out_specs=(P(None, "fsdp"), P(("fsdp", "dp"))),
        check_vma=False,
    )
```

time: 181 us -> 72.3 us (0.40)
  waiting for transfers between devices: 90.4 us -> 0 us
  Pallas kernels: 0 us -> 65.8 us
  blocking collectives: 37.2 us -> 0 us
  matrix products: 24.6 us -> 0 us
  between operations: 18.5 us -> 1.3 us
  other arithmetic: 7.1 us -> 0 us
  local copies, waits for them, and re-layouts: 2.09 us -> 4.85 us
    pallas_call x0 -> x2, Pallas kernels: none -> 65.8 us  [the longest x1 60.8 us: shards(): pl.pallas_call(functools.partial(kernel, nf, nd), out_shape=(jax.ShapeDty...]
    reduce_scatter x2 -> x0, waiting for transfers between devices: 47.5 us -> none  [the longest x1 23.9 us: shards(): lax.psum_scatter(both, 'fsdp', scatter_dimension=0, tiled=True)]
    all_gather x3 -> x0, waiting for transfers between devices: 42.4 us -> none  [the longest x1 22.1 us: shards(): seconds1 = lax.all_gather(second, 'dp', axis=0, tiled=True)]
    all_gather x3 -> x0, blocking collectives: 27.4 us -> none  [the longest x1 9.91 us: shards(): gathered = lax.all_gather(normed_rows, 'fsdp', axis=0, tiled=True)]
    dot_general x14 -> x0, matrix products: 24.6 us -> none  [the longest x10 14.4 us: dot32(): return jnp.dot(a, b, preferred_element_type=jnp.float32)]
    unnamed x1 -> x0, blocking collectives: 9.8 us -> none
    convert_element_type x5 -> x0, other arithmetic: 3.34 us -> none  [the longest x1 0.86 us: attend(): normed_rows = (hidden * lax.rsqrt(jnp.mean(hidden * hidden, -1, keepdims=...]
    unnamed x23 -> x12, local copies, waits for them, and re-layouts: 1.88 us -> 4.34 us
  transfers between devices with their start and end apart: 5 -> 0, of which waited for: 4 -> 0; matrix products, arithmetic and copies ran while one was open for 3% -> 0% of each run, Pallas kernels for 0% -> 0%
where the time goes in v2:
time: 72.3 us; the launch traced here: 72 us
  Pallas kernels  65.8 us (91%)
  local copies, waits for them, and re-layouts  4.85 us (7%)
  between operations  1.3 us (2%)
    pallas_call x1, Pallas kernels, shards(): pl.pallas_call(functools.partial(kernel, nf, nd), out_shape=(jax.ShapeDty...  60.8 us
    pallas_call x1, Pallas kernels, shards(): pl.pallas_call(functools.partial(finish, total), out_shape=jax.ShapeDtype...  5.05 us
    unnamed x12, local copies, waits for them, and re-layouts  4.34 us

profile of v2, /device:TPU:0, one launch (start us, length us, event | category | flops | bytes accessed | tf_op | source)
XLA Modules:
  0.0 72.0 jit_solution(4070210946319652059)
XLA Ops:
  1.3 0.0 copy-start.2
  1.3 0.9 %copy-done.2 = bf16[2,1,256,256]{3,2,1,0:T(8,128)(2,1)S(1)} copy-done((bf16[2,1,256,256]{3,2,1,0:T(8,128)(2,1)S(1)}, bf16[2,1,256,256]{3,2,1,0:T(8,128)(2,1)}, u32[]{:S(2)}) %copy-start.2) | copy-done | bytes 262168
  2.2 0.0 copy-start.3
  2.2 0.8 %copy-done.3 = bf16[16,1024]{1,0:T(8,128)(2,1)S(1)} copy-done((bf16[16,1024]{1,0:T(8,128)(2,1)S(1)}, bf16[16,1024]{1,0:T(8,128)(2,1)}, u32[]{:S(2)}) %copy-start.3) | copy-done | bytes 32792
  3.0 0.0 copy-start.4
  3.0 0.8 %copy-done.4 = bf16[16,1024]{1,0:T(8,128)(2,1)S(1)} copy-done((bf16[16,1024]{1,0:T(8,128)(2,1)S(1)}, bf16[16,1024]{1,0:T(8,128)(2,1)}, u32[]{:S(2)}) %copy-start.4) | copy-done | bytes 32792
  3.7 0.0 copy-start.5
  3.7 0.7 copy-done.5
  4.4 0.0 copy-start
  4.4 60.8 %lissa.1 = (bf16[512,1024]{1,0:T(8,128)(2,1)S(1)}, bf16[512,1024]{1,0:T(8,128)(2,1)}, f32[8,128]{1,0:T(8,128)S(1)}) custom-call(bf16[16,1024]{1,0:T(8,128)(2,1)S(1)} %copy-done.3, bf16[16,1024]{1,0:T(8,128)(2,1)S(1)} %copy-done.4, bf16[2,1,256,256]{3,2,1,0:T(8,128)(2,1)S(1)} %copy-done.2, s32[1]{0:T(128)S(6)} %copy.10.flow, s32[1,16]{1,0:T(1,128)S(1)} %bitcast.2, ...), custom_call_target="tpu_custom_call" | custom-call | tf_op jit(solution)/shard_map/lissa/pallas_call | solution.py:329
  65.2 0.5 slice.3
  65.7 0.0 copy-done
  65.7 0.0 copy-start.1
  65.7 1.2 %copy-done.1 = bf16[512,1024]{1,0:T(8,128)(2,1)S(1)} copy-done((bf16[512,1024]{1,0:T(8,128)(2,1)S(1)}, bf16[512,1024]{1,0:T(8,128)(2,1)}, u32[]{:S(2)}) %copy-start.1) | copy-done | bytes 1048600
  66.9 5.1 %finish.1 = f32[1024,1024]{1,0:T(8,128)} custom-call(bf16[512,1024]{1,0:T(8,128)(2,1)S(1)} %get-tuple-element.5.every, bf16[512,1024]{1,0:T(8,128)(2,1)S(1)} %copy-done.1, f32[1024,1024]{1,0:T(8,128)S(1)} %copy-done), custom_call_target="tpu_custom_call" | custom-call | tf_op jit(solution)/shard_map/finish/pallas_call | solution.py:377
Async XLA Ops:
  1.3 1.0 %copy-start.2 = (bf16[2,1,256,256]{3,2,1,0:T(8,128)(2,1)S(1)}, bf16[2,1,256,256]{3,2,1,0:T(8,128)(2,1)}, u32[]{:S(2)}) copy-start(bf16[2,1,256,256]{3,2,1,0:T(8,128)(2,1)} %kv.1) | copy-start | bytes 786436
  2.2 0.8 %copy-start.3 = (bf16[16,1024]{1,0:T(8,128)(2,1)S(1)}, bf16[16,1024]{1,0:T(8,128)(2,1)}, u32[]{:S(2)}) copy-start(bf16[16,1024]{1,0:T(8,128)(2,1)} %noise.1) | copy-start | bytes 98308
  3.0 0.8 %copy-start.4 = (bf16[16,1024]{1,0:T(8,128)(2,1)S(1)}, bf16[16,1024]{1,0:T(8,128)(2,1)}, u32[]{:S(2)}) copy-start(bf16[16,1024]{1,0:T(8,128)(2,1)} %action.1) | copy-start | bytes 98308
  3.7 0.7 copy-start.5
  4.4 61.3 %copy-start = (f32[1024,1024]{1,0:T(8,128)S(1)}, f32[1024,1024]{1,0:T(8,128)}, u32[]{:S(2)}) copy-start(f32[1024,1024]{1,0:T(8,128)} %grad.1) | copy-start | bytes 12582916
  65.7 1.2 %copy-start.1 = (bf16[512,1024]{1,0:T(8,128)(2,1)S(1)}, bf16[512,1024]{1,0:T(8,128)(2,1)}, u32[]{:S(2)}) copy-start(bf16[512,1024]{1,0:T(8,128)(2,1)} %get-tuple-element.6.mix) | copy-start | bytes 3145732

commit v3 on v2

--- a/solution.py
+++ b/solution.py
@@ -310,6 +310,359 @@
     keep_mix.wait()
 
 
+def spread(
+    nf, nd,
+    noise_h, action_h, kv_h, flow, mask_h, w_up_h, w_down_h, grad_h,
+    out, score,
+    noise, action, kv, mask, w_up, w_down, grad, every, flipped, seconds, gram,
+    slopes, curves, pulled, tan0, tan1, lhs, part, land0, land1, pair0, pair1,
+    resid, tally, tally_in,
+    load_sem, store_sem, f_send, f_recv, z_send, z_recv, x_send, x_recv, c_send, c_recv,
+):
+    acts, width = noise.shape
+    hid = w_up.shape[1]
+    rows = nf * acts
+    total = nd * rows
+    chips = nd // CORES
+    pack = CORES * rows
+    step = min(256, hid)
+    wide = min(256, width)
+    f = lax.axis_index("fsdp")
+    d = lax.axis_index("dp")
+    chip, core = d // CORES, d % CORES
+    sibling = chip * CORES + (1 - core)
+
+    def f_peer(k):
+        return lax.rem(f + k, nf)
+
+    def f_from(k):
+        return lax.rem(f + nf - k, nf)
+
+    def d_peer(k):
+        return lax.rem(chip + k, chips) * CORES + core
+
+    def chip_from(k):
+        return lax.rem(chip + chips - k, chips)
+
+    barrier = pltpu.get_barrier_semaphore()
+    for k in range(1, nf):
+        pl.semaphore_signal(barrier, inc=1, device_id=(f_peer(k), d), device_id_type=MESH)
+    for k in range(1, chips):
+        pl.semaphore_signal(barrier, inc=1, device_id=(f, d_peer(k)), device_id_type=MESH)
+    pl.semaphore_signal(barrier, inc=1, device_id=(f, sibling), device_id_type=MESH)
+
+    pairs = (
+        (noise_h, noise), (action_h, action), (kv_h, kv), (mask_h, mask),
+        (w_up_h, w_up), (grad_h, grad), (w_down_h, w_down),
+    )
+    loads = [pltpu.make_async_copy(src, dst, load_sem.at[i]) for i, (src, dst) in enumerate(pairs)]
+    for load in loads:
+        load.start()
+
+    def remote(src, dst, send, recv, who):
+        copy = pltpu.make_async_remote_copy(
+            src_ref=src, dst_ref=dst, send_sem=send, recv_sem=recv, device_id=who, device_id_type=MESH
+        )
+        copy.start()
+        return copy
+
+    sent = []
+
+    def scatter(phase, src, dst):
+        return [
+            remote(src(f_peer(k)), dst(k), f_send.at[phase, k], f_recv.at[phase, k], (f_peer(k), d))
+            for k in range(1, nf)
+        ]
+
+    def block(g, kk, k):
+        who = chip_from(kk) * CORES + core
+        if g == 1:
+            return pair0.at[who, :, tile(f_from(k), acts), :]
+        at = pl.ds(pl.multiple_of(who * rows + f_from(k) * acts, acts), acts)
+        return (every if g == 0 else pair1).at[at, :]
+
+    across, to_core, along = {}, {}, {}
+
+    def keep_copy(table, key, copy):
+        table[key] = copy
+        sent.append(copy)
+
+    def share(g, kk):
+        mine = block(g, kk, 0)
+        for k in range(1, nf):
+            keep_copy(across, (g, kk, k), remote(
+                mine, mine, x_send.at[g, kk, k], x_recv.at[g, kk, k], (f_peer(k), d)
+            ))
+        pass_on(g, kk, 0)
+
+    def pass_on(g, kk, k):
+        mine = block(g, kk, k)
+        keep_copy(to_core, (g, kk, k), remote(
+            mine, mine, c_send.at[g, kk, k], c_recv.at[g, kk, k], (f, sibling)
+        ))
+
+    def begin(g):
+        mine = block(g, 0, 0)
+        for k in range(1, chips):
+            keep_copy(along, (g, k), remote(
+                mine, mine, z_send.at[g, k], z_recv.at[g, k], (f, d_peer(k))
+            ))
+        share(g, 0)
+
+    def from_z(g):
+        for kk in range(1, chips):
+            along[g, kk].wait_recv()
+            share(g, kk)
+
+    def from_f(g, kk):
+        for k in range(1, nf):
+            across[g, kk, k].wait_recv()
+            pass_on(g, kk, k)
+
+    def from_core(g, kk):
+        for k in range(nf):
+            to_core[g, kk, k].wait_recv()
+
+    for load in loads[:4]:
+        load.wait()
+    normed, left = attend(noise, action, kv, flow)
+    resid[...] = left
+    own = pl.ds(pl.multiple_of(d * rows + f * acts, acts), acts)
+    every[own, :] = normed
+    lane = lax.broadcasted_iota(jnp.int32, (acts, acts), 1)
+    line = lax.broadcasted_iota(jnp.int32, (acts, acts), 0)
+    valid = jnp.sum(
+        jnp.where(lane == line, jnp.broadcast_to(mask[...].astype(F32), (acts, acts)), 0.0), -1, keepdims=True
+    )
+    pl.semaphore_wait(barrier, nf - 1 + chips)
+    begin(0)
+    group_at = tile(d, rows)
+
+    def first(at, cut):
+        group = every[at, :]
+        pre = dot32(group, w_up[:, cut])
+        tangent = dot32(group, grad[:, cut].astype(BF))
+        sig = 1.0 / (1.0 + jnp.exp(-pre))
+        slope = sig * (1.0 + pre * (1.0 - sig))
+        slopes[at, cut] = slope
+        curves[at, cut] = sig * (1.0 - sig) * (2.0 + pre * (1.0 - 2.0 * sig))
+        tan0[at, cut] = tangent
+        return pre * sig, slope * tangent
+
+    def first_own(i):
+        cut = tile(i, step)
+        active, linear = first(group_at, cut)
+        lhs[0:rows, cut] = active.astype(BF)
+        lhs[rows : 2 * rows, cut] = linear.astype(BF)
+
+    loads[4].wait()
+    loads[5].wait()
+    from_f(0, 0)
+    loop(hid // step, first_own)
+    from_z(0)
+    loads[6].wait()
+
+    def down(i):
+        cut = tile(i, wide)
+        part[:, cut] = dot32(lhs[...], w_down[:, cut]).astype(BF)
+
+    loop(width // wide, down)
+
+    def rows_of(p, q):
+        return pl.ds(pl.multiple_of(q * rows + p * acts, acts), acts)
+
+    outs = scatter(0, lambda p: part.at[rows_of(p, 0), :], lambda k: land0.at[k, 0:acts, :])
+    moves = scatter(1, lambda p: part.at[rows_of(p, 1), :], lambda k: land0.at[k, acts : 2 * acts, :])
+
+    def summed(copies, q, land, lo):
+        value = part[rows_of(f, q), :].astype(F32)
+        for k in range(1, nf):
+            copies[k - 1].wait_recv()
+            value = value + land[k, lo : lo + acts, :].astype(F32)
+        return value
+
+    def chunk(kk):
+        return tile(chip_from(kk), pack)
+
+    def rest(kk):
+        from_core(0, kk)
+
+        def body(i):
+            first(chunk(kk), tile(i, step))
+
+        loop(hid // step, body)
+
+    rest(0)
+    here = tile(f, acts)
+    pair0[d, 0, here, :] = (valid * (resid[...] + summed(outs, 0, land0, 0))).astype(BF)
+    pair0[d, 1, here, :] = (valid * summed(moves, 1, land0, acts)).astype(BF)
+    begin(1)
+    for kk in range(1, chips):
+        from_f(0, kk)
+    rest(1)
+    from_z(1)
+    for kk in range(2, chips):
+        rest(kk)
+    from_f(1, 0)
+
+    def grams(i):
+        cut = tile(i, pack)
+        gram[cut, :] = (dot_t(every[cut, :], every[...]) / total).astype(BF)
+
+    loop(chips, grams)
+
+    def flip(i):
+        cut = tile(i, wide)
+        flipped[cut, :] = every[:, cut].T
+
+    loop(width // wide, flip)
+
+    def bend(kk):
+        base = chip_from(kk) * CORES
+
+        def body(i):
+            cut = tile(i, step)
+            tokens = pair0[pl.ds(base, CORES)].reshape(2 * pack, width)
+            both = dot_t(tokens, w_down[cut, :])
+            for c in range(CORES):
+                at = tile(base + c, rows)
+                pull = both[2 * c * rows : (2 * c + 1) * rows]
+                push = both[(2 * c + 1) * rows : (2 * c + 2) * rows]
+                pulled[at, cut] = pull
+                seconds[0, at, cut] = (
+                    push * slopes[at, cut] + pull * curves[at, cut] * tan0[at, cut]
+                ).astype(BF)
+
+        loop(hid // step, body)
+
+    for kk in range(chips):
+        if kk + 1 < chips:
+            from_f(1, kk + 1)
+        from_core(1, kk)
+        bend(kk)
+
+    def again(at, cut):
+        tangent = (1.0 + keep) * tan0[at, cut] - dot32(gram[at, :], seconds[0, :, cut])
+        tan1[at, cut] = tangent
+        return tangent
+
+    def again_own(i):
+        cut = tile(i, step)
+        lhs[0:rows, cut] = (slopes[group_at, cut] * again(group_at, cut)).astype(BF)
+
+    loop(hid // step, again_own)
+    for copy in outs + moves:
+        copy.wait_send()
+
+    def down_again(i):
+        cut = tile(i, wide)
+        part[0:rows, cut] = dot32(lhs[0:rows, :], w_down[:, cut]).astype(BF)
+
+    loop(width // wide, down_again)
+    moves1 = scatter(2, lambda p: part.at[rows_of(p, 0), :], lambda k: land1.at[k])
+    sent.extend(moves1)
+
+    def again_all(i):
+        again(slice(None), tile(i, step))
+
+    loop(hid // step, again_all)
+    pair1[own, :] = (valid * summed(moves1, 0, land1, 0)).astype(BF)
+    begin(2)
+
+    def settle(i):
+        cut = tile(i, wide)
+        change = dot32(flipped[cut, :], seconds[0])
+        grad[cut, :] = (1.0 + keep + keep * keep) * grad[cut, :] - (keep / total) * change
+
+    half = max(1, width // wide // 2)
+    pl.loop(0, half)(settle)
+    from_z(2)
+    pl.loop(half, width // wide)(settle)
+    from_f(2, 0)
+
+    def bend_again(kk):
+        at = chunk(kk)
+
+        def body(i):
+            cut = tile(i, step)
+            both = dot_t(pair1[at, :], w_down[cut, :])
+            seconds[1, at, cut] = (
+                both * slopes[at, cut] + pulled[at, cut] * curves[at, cut] * tan1[at, cut]
+            ).astype(BF)
+
+        loop(hid // step, body)
+
+    for kk in range(chips):
+        if kk + 1 < chips:
+            from_f(2, kk + 1)
+        from_core(2, kk)
+        bend_again(kk)
+
+    def rate(i, terms):
+        cut = tile(i, step)
+        projected = tan0[group_at, cut] + keep * tan1[group_at, cut]
+        projected = projected - dot32(gram[group_at, :], seconds[1, :, cut])
+        return terms + projected * (pulled[group_at, cut] * slopes[group_at, cut])
+
+    terms = lax.fori_loop(0, hid // step, rate, jnp.zeros((rows, step), F32))
+    for p in range(nf):
+        one = jnp.sum(terms[p * acts : (p + 1) * acts], 0, keepdims=True)
+        tally[p] = jnp.broadcast_to(jnp.sum(one, -1, keepdims=True), tally.shape[1:])
+    votes = scatter(3, lambda p: tally.at[p], lambda k: tally_in.at[k])
+    sent.extend(votes)
+    stores = []
+    for i in range(width // wide):
+        cut = pl.ds(i * wide, wide)
+        grad[cut, :] = grad[cut, :] - dot32(flipped[cut, :], seconds[1]) / total
+        stores.append(pltpu.make_async_copy(grad.at[cut, :], out.at[cut, :], store_sem.at[i]))
+        stores[-1].start()
+    value = tally[f]
+    for k in range(1, nf):
+        votes[k - 1].wait_recv()
+        value = value + tally_in[k]
+    score[...] = -value / (acts * math.sqrt(width * hid * nf))
+    for copy in sent:
+        copy.wait_send()
+    for store in stores:
+        store.wait()
+
+
+def spread_call(nf, nd, noise, action, kv, flow, mask, w_up, w_down, grad):
+    acts, width = noise.shape
+    hid = w_up.shape[1]
+    rows = nf * acts
+    total = nd * rows
+    chips = nd // CORES
+    vmem = pl.BlockSpec(memory_space=pltpu.VMEM)
+    anywhere = pl.BlockSpec(memory_space=pl.ANY)
+    dma = pltpu.SemaphoreType.DMA
+    far = pl.BlockSpec(memory_space=pltpu.HBM)
+    half, full = (lambda *s: pltpu.VMEM(s, BF)), (lambda *s: pltpu.VMEM(s, F32))
+    vector, score = pl.pallas_call(
+        functools.partial(spread, nf, nd),
+        out_shape=(jax.ShapeDtypeStruct((width, hid), F32), jax.ShapeDtypeStruct((8, 128), F32)),
+        in_specs=[far] * 3 + [pl.BlockSpec(memory_space=pltpu.SMEM)] + [far] * 4,
+        out_specs=(anywhere, vmem),
+        scratch_shapes=[
+            half(acts, width), half(acts, width), half(*kv.shape), pltpu.VMEM((1, acts), jnp.int32),
+            half(width, hid), half(hid, width), full(width, hid),
+            half(total, width), half(width, total), half(2, total, hid), half(total, total),
+        ] + [full(total, hid)] * 5 + [
+            half(2 * rows, hid), half(2 * rows, width), half(nf, 2 * acts, width), half(nf, acts, width),
+            half(nd, 2, rows, width), half(total, width),
+            full(acts, width), full(nf, 8, 128), full(nf, 8, 128),
+            dma((7,)), dma((max(1, width // 256),)), dma((4, nf)), dma((4, nf)),
+            dma((3, chips)), dma((3, chips)), dma((3, chips, nf)), dma((3, chips, nf)),
+            dma((3, chips, nf)), dma((3, chips, nf)),
+        ],
+        compiler_params=pltpu.CompilerParams(
+            collective_id=0, has_side_effects=True, vmem_limit_bytes=60 * 1024 * 1024
+        ),
+        name="lissa",
+    )(noise, action, kv, flow, mask.reshape(1, acts), w_up, w_down, grad)
+    return vector, score[0, 0:1]
+
+
 def finish(total, every, mix, grad, out):
     change = lax.dot_general(
         every[...], mix[...], (((0,), (0,)), ((), ())), preferred_element_type=F32
@@ -322,6 +675,8 @@
     hid = w_up.shape[1]
     rows = nf * acts
     total = nd * rows
+    if total <= 512:
+        return spread_call(nf, nd, noise, action, kv, flow, mask, w_up, w_down, grad)
     vmem = pl.BlockSpec(memory_space=pltpu.VMEM)
     anywhere = pl.BlockSpec(memory_space=pl.ANY)
     dma = pltpu.SemaphoreType.DMA

time: 72.3 us -> 68.1 us (0.942)
  Pallas kernels: 65.8 us -> 60.6 us
  local copies, waits for them, and re-layouts: 4.85 us -> 5.97 us
    pallas_call x2 -> x1, Pallas kernels: 65.8 us -> 60.6 us  [spread_call(): pl.pallas_call(functools.partial(spread, nf, nd), out_shape=(jax.ShapeDty...]
    unnamed x12 -> x1, local copies, waits for them, and re-layouts: 4.34 us -> 4.79 us
where the time goes in v3:
time: 68.1 us; the launch traced here: 67.9 us
  Pallas kernels  60.6 us (89%)
  local copies, waits for them, and re-layouts  5.97 us (9%)
  between operations  1.29 us (2%)
    pallas_call x1, Pallas kernels, spread_call(): pl.pallas_call(functools.partial(spread, nf, nd), out_shape=(jax.ShapeDty...  60.6 us
    unnamed x1, local copies, waits for them, and re-layouts  4.79 us

profile of v3, /device:TPU:0, one launch (start us, length us, event | category | flops | bytes accessed | tf_op | source)
XLA Modules:
  0.0 67.9 jit_solution(15488871146352952752)
XLA Ops:
  1.3 60.6 %lissa.1 = (f32[1024,1024]{1,0:T(8,128)}, f32[8,128]{1,0:T(8,128)}) custom-call(bf16[16,1024]{1,0:T(8,128)(2,1)} %noise_h.1, bf16[16,1024]{1,0:T(8,128)(2,1)} %action_h.1, bf16[2,1,256,256]{3,2,1,0:T(8,128)(2,1)} %kv_h.1, s32[1]{0:T(128)S(6)} %copy.11.flow, s32[1,16]{1,0:T(1,128)} %bitcast.2, bf16[1024,1024]{1,0:T(8,128)(2,1)} %w_up_h.1, ...), custom_call_target="tpu_custom_call" | custom-call | tf_op jit(solution)/shard_map/lissa/pallas_call | solution.py:641
  61.9 1.2 %slice.3 = f32[1,1]{1,0:T(1,128)} slice(f32[8,128]{1,0:T(8,128)} %get-tuple-element.5), slice={[0:1], [0:1]} | slice | bytes 8 | tf_op jit(solution)/shard_map/slice | solution.py:663
  63.1 4.8 %copy.12 = f32[1024,1024]{1,0:T(8,128)} copy(f32[1024,1024]{1,0:T(8,128)} %get-tuple-element.8) | data formatting | bytes 8388608

commit v4 on v3

--- a/solution.py
+++ b/solution.py
@@ -314,7 +314,7 @@
     nf, nd,
     noise_h, action_h, kv_h, flow, mask_h, w_up_h, w_down_h, grad_h,
     out, score,
-    noise, action, kv, mask, w_up, w_down, grad, every, flipped, seconds, gram,
+    noise, action, kv, mask, w_up, w_down, grad, gradb, every, flipped, seconds, gram,
     slopes, curves, pulled, tan0, tan1, lhs, part, land0, land1, pair0, pair1,
     resid, tally, tally_in,
     load_sem, store_sem, f_send, f_recv, z_send, z_recv, x_send, x_recv, c_send, c_recv,
@@ -393,13 +393,6 @@
             keep_copy(across, (g, kk, k), remote(
                 mine, mine, x_send.at[g, kk, k], x_recv.at[g, kk, k], (f_peer(k), d)
             ))
-        pass_on(g, kk, 0)
-
-    def pass_on(g, kk, k):
-        mine = block(g, kk, k)
-        keep_copy(to_core, (g, kk, k), remote(
-            mine, mine, c_send.at[g, kk, k], c_recv.at[g, kk, k], (f, sibling)
-        ))
 
     def begin(g):
         mine = block(g, 0, 0)
@@ -417,11 +410,14 @@
     def from_f(g, kk):
         for k in range(1, nf):
             across[g, kk, k].wait_recv()
-            pass_on(g, kk, k)
+        who = chip_from(kk) * CORES + core
+        mine = pair0.at[who] if g == 1 else (every if g == 0 else pair1).at[tile(who, rows), :]
+        keep_copy(to_core, (g, kk), remote(
+            mine, mine, c_send.at[g, kk], c_recv.at[g, kk], (f, sibling)
+        ))
 
     def from_core(g, kk):
-        for k in range(nf):
-            to_core[g, kk, k].wait_recv()
+        to_core[g, kk].wait_recv()
 
     for load in loads[:4]:
         load.wait()
@@ -441,7 +437,7 @@
     def first(at, cut):
         group = every[at, :]
         pre = dot32(group, w_up[:, cut])
-        tangent = dot32(group, grad[:, cut].astype(BF))
+        tangent = dot32(group, gradb[:, cut])
         sig = 1.0 / (1.0 + jnp.exp(-pre))
         slope = sig * (1.0 + pre * (1.0 - sig))
         slopes[at, cut] = slope
@@ -455,11 +451,19 @@
         lhs[0:rows, cut] = active.astype(BF)
         lhs[rows : 2 * rows, cut] = linear.astype(BF)
 
+    loads[5].wait()
+
+    def narrow(i):
+        cut = tile(i, wide)
+        gradb[cut, :] = grad[cut, :].astype(BF)
+
+    loop(width // wide, narrow)
     loads[4].wait()
-    loads[5].wait()
     from_f(0, 0)
-    loop(hid // step, first_own)
+    first_own(0)
     from_z(0)
+    if hid > step:
+        pl.loop(1, hid // step)(first_own)
     loads[6].wait()
 
     def down(i):
@@ -613,7 +617,7 @@
     stores = []
     for i in range(width // wide):
         cut = pl.ds(i * wide, wide)
-        grad[cut, :] = grad[cut, :] - dot32(flipped[cut, :], seconds[1]) / total
+        grad[cut, :] = grad[cut, :] - dot32(flipped[cut, :], seconds[1]) * (1.0 / total)
         stores.append(pltpu.make_async_copy(grad.at[cut, :], out.at[cut, :], store_sem.at[i]))
         stores[-1].start()
     value = tally[f]
@@ -627,6 +631,22 @@
         store.wait()
 
 
+def hand_out(held, tally, out, score, sem):
+    parts = sem.shape[0]
+    high = out.shape[0] // parts
+    copies = [
+        pltpu.make_async_copy(
+            held.at[pl.ds(i * high, high), :], out.at[pl.ds(i * high, high), :], sem.at[i]
+        )
+        for i in range(parts)
+    ]
+    for copy in copies:
+        copy.start()
+    score[0] = tally[0, 0]
+    for copy in copies:
+        copy.wait()
+
+
 def spread_call(nf, nd, noise, action, kv, flow, mask, w_up, w_down, grad):
     acts, width = noise.shape
     hid = w_up.shape[1]
@@ -636,16 +656,15 @@
     vmem = pl.BlockSpec(memory_space=pltpu.VMEM)
     anywhere = pl.BlockSpec(memory_space=pl.ANY)
     dma = pltpu.SemaphoreType.DMA
-    far = pl.BlockSpec(memory_space=pltpu.HBM)
     half, full = (lambda *s: pltpu.VMEM(s, BF)), (lambda *s: pltpu.VMEM(s, F32))
     vector, score = pl.pallas_call(
         functools.partial(spread, nf, nd),
         out_shape=(jax.ShapeDtypeStruct((width, hid), F32), jax.ShapeDtypeStruct((8, 128), F32)),
-        in_specs=[far] * 3 + [pl.BlockSpec(memory_space=pltpu.SMEM)] + [far] * 4,
+        in_specs=[anywhere] * 3 + [pl.BlockSpec(memory_space=pltpu.SMEM)] + [anywhere] * 4,
         out_specs=(anywhere, vmem),
         scratch_shapes=[
             half(acts, width), half(acts, width), half(*kv.shape), pltpu.VMEM((1, acts), jnp.int32),
-            half(width, hid), half(hid, width), full(width, hid),
+            half(width, hid), half(hid, width), full(width, hid), half(width, hid),
             half(total, width), half(width, total), half(2, total, hid), half(total, total),
         ] + [full(total, hid)] * 5 + [
             half(2 * rows, hid), half(2 * rows, width), half(nf, 2 * acts, width), half(nf, acts, width),
@@ -653,14 +672,22 @@
             full(acts, width), full(nf, 8, 128), full(nf, 8, 128),
             dma((7,)), dma((max(1, width // 256),)), dma((4, nf)), dma((4, nf)),
             dma((3, chips)), dma((3, chips)), dma((3, chips, nf)), dma((3, chips, nf)),
-            dma((3, chips, nf)), dma((3, chips, nf)),
+            dma((3, chips)), dma((3, chips)),
         ],
         compiler_params=pltpu.CompilerParams(
             collective_id=0, has_side_effects=True, vmem_limit_bytes=60 * 1024 * 1024
         ),
         name="lissa",
     )(noise, action, kv, flow, mask.reshape(1, acts), w_up, w_down, grad)
-    return vector, score[0, 0:1]
+    return pl.pallas_call(
+        hand_out,
+        out_shape=(jax.ShapeDtypeStruct((width, hid), F32), jax.ShapeDtypeStruct((1,), F32)),
+        in_specs=[anywhere, vmem],
+        out_specs=(anywhere, pl.BlockSpec(memory_space=pltpu.SMEM)),
+        scratch_shapes=[dma((4,))],
+        compiler_params=pltpu.CompilerParams(vmem_limit_bytes=60 * 1024 * 1024),
+        name="hand_out",
+    )(vector, score)
 
 
 def finish(total, every, mix, grad, out):

time: 68.1 us -> 190 us (2.79)
  Pallas kernels: 60.6 us -> 188 us
  local copies, waits for them, and re-layouts: 5.97 us -> 0 us
    pallas_call x0 -> x1, Pallas kernels: none -> 129 us  [spread_call(): pl.pallas_call(hand_out, out_shape=(jax.ShapeDtypeStruct((width, hid), F3...]
    unnamed x1 -> x0, local copies, waits for them, and re-layouts: 4.79 us -> none
where the time goes in v4:
time: 190 us
  Pallas kernels  188 us (99%)
    pallas_call x1, Pallas kernels, spread_call(): pl.pallas_call(hand_out, out_shape=(jax.ShapeDtypeStruct((width, hid), F3...  129 us
    pallas_call x1, Pallas kernels, spread_call(): pl.pallas_call(functools.partial(spread, nf, nd), out_shape=(jax.ShapeDty...  58.9 us

profile of v4, /device:TPU:0, one launch (start us, length us, event | category | flops | bytes accessed | tf_op | source)
XLA Modules:
  0.0 189.6 jit_solution(14098484825059098744)
XLA Ops:
  1.3 58.9 %lissa.1 = (f32[1024,1024]{1,0:T(8,128)}, f32[8,128]{1,0:T(8,128)}) custom-call(bf16[16,1024]{1,0:T(8,128)(2,1)} %noise_h.1, bf16[16,1024]{1,0:T(8,128)(2,1)} %action_h.1, bf16[2,1,256,256]{3,2,1,0:T(8,128)(2,1)} %kv_h.1, s32[1]{0:T(128)S(6)} %copy.10.flow, s32[1,16]{1,0:T(1,128)} %bitcast.1, bf16[1024,1024]{1,0:T(8,128)(2,1)} %w_up_h.1, ...), custom_call_target="tpu_custom_call" | custom-call | tf_op jit(solution)/shard_map/lissa/pallas_call | solution.py:660
  60.2 129.4 %hand_out.1 = (f32[1024,1024]{1,0:T(8,128)}, f32[1]{0:T(128)}) custom-call(f32[1024,1024]{1,0:T(8,128)} %get-tuple-element.4.held, f32[8,128]{1,0:T(8,128)} %get-tuple-element.5.tally), custom_call_target="tpu_custom_call" | custom-call | tf_op jit(solution)/shard_map/hand_out/pallas_call | solution.py:682

commit v5 on v4

--- a/solution.py
+++ b/solution.py
@@ -324,7 +324,7 @@
     rows = nf * acts
     total = nd * rows
     chips = nd // CORES
-    pack = CORES * rows
+    pack = chips * rows
     step = min(256, hid)
     wide = min(256, width)
     f = lax.axis_index("fsdp")
@@ -375,9 +375,11 @@
         ]
 
     def block(g, kk, k):
-        who = chip_from(kk) * CORES + core
+        who = chip_from(kk)
         if g == 1:
             return pair0.at[who, :, tile(f_from(k), acts), :]
+        if g == 0:
+            who = core * chips + who
         at = pl.ds(pl.multiple_of(who * rows + f_from(k) * acts, acts), acts)
         return (every if g == 0 else pair1).at[at, :]
 
@@ -410,20 +412,23 @@
     def from_f(g, kk):
         for k in range(1, nf):
             across[g, kk, k].wait_recv()
-        who = chip_from(kk) * CORES + core
-        mine = pair0.at[who] if g == 1 else (every if g == 0 else pair1).at[tile(who, rows), :]
+
+    def swap(g, kk):
+        at = tile(core * chips + chip_from(kk), rows)
+        mine = every.at[at, :] if g == 0 else seconds.at[g - 1, at, :]
         keep_copy(to_core, (g, kk), remote(
             mine, mine, c_send.at[g, kk], c_recv.at[g, kk], (f, sibling)
         ))
 
-    def from_core(g, kk):
-        to_core[g, kk].wait_recv()
+    def swapped(g):
+        for kk in range(chips):
+            to_core[g, kk].wait_recv()
 
     for load in loads[:4]:
         load.wait()
     normed, left = attend(noise, action, kv, flow)
     resid[...] = left
-    own = pl.ds(pl.multiple_of(d * rows + f * acts, acts), acts)
+    own = pl.ds(pl.multiple_of((core * chips + chip) * rows + f * acts, acts), acts)
     every[own, :] = normed
     lane = lax.broadcasted_iota(jnp.int32, (acts, acts), 1)
     line = lax.broadcasted_iota(jnp.int32, (acts, acts), 0)
@@ -432,10 +437,10 @@
     )
     pl.semaphore_wait(barrier, nf - 1 + chips)
     begin(0)
-    group_at = tile(d, rows)
-
-    def first(at, cut):
-        group = every[at, :]
+    group_at = tile(chip, rows)
+
+    def first(whole, at, cut):
+        group = every[whole, :]
         pre = dot32(group, w_up[:, cut])
         tangent = dot32(group, gradb[:, cut])
         sig = 1.0 / (1.0 + jnp.exp(-pre))
@@ -447,7 +452,7 @@
 
     def first_own(i):
         cut = tile(i, step)
-        active, linear = first(group_at, cut)
+        active, linear = first(tile(core * chips + chip, rows), group_at, cut)
         lhs[0:rows, cut] = active.astype(BF)
         lhs[rows : 2 * rows, cut] = linear.astype(BF)
 
@@ -460,6 +465,7 @@
     loop(width // wide, narrow)
     loads[4].wait()
     from_f(0, 0)
+    swap(0, 0)
     first_own(0)
     from_z(0)
     if hid > step:
@@ -485,35 +491,28 @@
             value = value + land[k, lo : lo + acts, :].astype(F32)
         return value
 
-    def chunk(kk):
-        return tile(chip_from(kk), pack)
-
-    def rest(kk):
-        from_core(0, kk)
-
-        def body(i):
-            first(chunk(kk), tile(i, step))
-
-        loop(hid // step, body)
-
-    rest(0)
     here = tile(f, acts)
-    pair0[d, 0, here, :] = (valid * (resid[...] + summed(outs, 0, land0, 0))).astype(BF)
-    pair0[d, 1, here, :] = (valid * summed(moves, 1, land0, acts)).astype(BF)
+    pair0[chip, 0, here, :] = (valid * (resid[...] + summed(outs, 0, land0, 0))).astype(BF)
+    pair0[chip, 1, here, :] = (valid * summed(moves, 1, land0, acts)).astype(BF)
     begin(1)
     for kk in range(1, chips):
         from_f(0, kk)
-    rest(1)
+        swap(0, kk)
+
+    def rest(i):
+        first(tile(core, pack), slice(None), tile(i, step))
+
+    rest(0)
     from_z(1)
-    for kk in range(2, chips):
-        rest(kk)
-    from_f(1, 0)
+    if hid > step:
+        pl.loop(1, hid // step)(rest)
+    swapped(0)
 
     def grams(i):
         cut = tile(i, pack)
-        gram[cut, :] = (dot_t(every[cut, :], every[...]) / total).astype(BF)
-
-    loop(chips, grams)
+        gram[:, cut] = (dot_t(every[tile(core, pack), :], every[cut, :]) * (1.0 / total)).astype(BF)
+
+    loop(CORES, grams)
 
     def flip(i):
         cut = tile(i, wide)
@@ -522,28 +521,25 @@
     loop(width // wide, flip)
 
     def bend(kk):
-        base = chip_from(kk) * CORES
+        at = tile(chip_from(kk), rows)
+        whole = tile(core * chips + chip_from(kk), rows)
 
         def body(i):
             cut = tile(i, step)
-            tokens = pair0[pl.ds(base, CORES)].reshape(2 * pack, width)
-            both = dot_t(tokens, w_down[cut, :])
-            for c in range(CORES):
-                at = tile(base + c, rows)
-                pull = both[2 * c * rows : (2 * c + 1) * rows]
-                push = both[(2 * c + 1) * rows : (2 * c + 2) * rows]
-                pulled[at, cut] = pull
-                seconds[0, at, cut] = (
-                    push * slopes[at, cut] + pull * curves[at, cut] * tan0[at, cut]
-                ).astype(BF)
+            both = dot_t(pair0[chip_from(kk)].reshape(2 * rows, width), w_down[cut, :])
+            pull = both[0:rows]
+            pulled[at, cut] = pull
+            seconds[0, whole, cut] = (
+                both[rows : 2 * rows] * slopes[at, cut] + pull * curves[at, cut] * tan0[at, cut]
+            ).astype(BF)
 
         loop(hid // step, body)
 
     for kk in range(chips):
-        if kk + 1 < chips:
-            from_f(1, kk + 1)
-        from_core(1, kk)
+        from_f(1, kk)
         bend(kk)
+        swap(1, kk)
+    swapped(1)
 
     def again(at, cut):
         tangent = (1.0 + keep) * tan0[at, cut] - dot32(gram[at, :], seconds[0, :, cut])
@@ -570,7 +566,7 @@
         again(slice(None), tile(i, step))
 
     loop(hid // step, again_all)
-    pair1[own, :] = (valid * summed(moves1, 0, land1, 0)).astype(BF)
+    pair1[pl.ds(pl.multiple_of(chip * rows + f * acts, acts), acts), :] = (valid * summed(moves1, 0, land1, 0)).astype(BF)
     begin(2)
 
     def settle(i):
@@ -582,25 +578,25 @@
     pl.loop(0, half)(settle)
     from_z(2)
     pl.loop(half, width // wide)(settle)
-    from_f(2, 0)
 
     def bend_again(kk):
-        at = chunk(kk)
+        at = tile(chip_from(kk), rows)
+        whole = tile(core * chips + chip_from(kk), rows)
 
         def body(i):
             cut = tile(i, step)
             both = dot_t(pair1[at, :], w_down[cut, :])
-            seconds[1, at, cut] = (
+            seconds[1, whole, cut] = (
                 both * slopes[at, cut] + pulled[at, cut] * curves[at, cut] * tan1[at, cut]
             ).astype(BF)
 
         loop(hid // step, body)
 
     for kk in range(chips):
-        if kk + 1 < chips:
-            from_f(2, kk + 1)
-        from_core(2, kk)
+        from_f(2, kk)
         bend_again(kk)
+        swap(2, kk)
+    swapped(2)
 
     def rate(i, terms):
         cut = tile(i, step)
@@ -631,20 +627,25 @@
         store.wait()
 
 
-def hand_out(held, tally, out, score, sem):
-    parts = sem.shape[0]
+def hand_out(held, tally, out, score, stage, sems):
+    parts = sems.shape[1]
     high = out.shape[0] // parts
-    copies = [
-        pltpu.make_async_copy(
-            held.at[pl.ds(i * high, high), :], out.at[pl.ds(i * high, high), :], sem.at[i]
-        )
-        for i in range(parts)
-    ]
-    for copy in copies:
-        copy.start()
+
+    def move(i, to):
+        at = pl.ds(i * high, high)
+        src, dst = (stage, out) if to else (held, stage)
+        return pltpu.make_async_copy(src.at[at, :], dst.at[at, :], sems.at[to, i])
+
+    loads = [move(i, 0) for i in range(parts)]
+    stores = [move(i, 1) for i in range(parts)]
+    for load in loads:
+        load.start()
     score[0] = tally[0, 0]
-    for copy in copies:
-        copy.wait()
+    for load, store in zip(loads, stores):
+        load.wait()
+        store.start()
+    for store in stores:
+        store.wait()
 
 
 def spread_call(nf, nd, noise, action, kv, flow, mask, w_up, w_down, grad):
@@ -665,10 +666,10 @@
         scratch_shapes=[
             half(acts, width), half(acts, width), half(*kv.shape), pltpu.VMEM((1, acts), jnp.int32),
             half(width, hid), half(hid, width), full(width, hid), half(width, hid),
-            half(total, width), half(width, total), half(2, total, hid), half(total, total),
-        ] + [full(total, hid)] * 5 + [
+            half(total, width), half(width, total), half(2, total, hid), half(total // CORES, total),
+        ] + [full(total // CORES, hid)] * 5 + [
             half(2 * rows, hid), half(2 * rows, width), half(nf, 2 * acts, width), half(nf, acts, width),
-            half(nd, 2, rows, width), half(total, width),
+            half(chips, 2, rows, width), half(total // CORES, width),
             full(acts, width), full(nf, 8, 128), full(nf, 8, 128),
             dma((7,)), dma((max(1, width // 256),)), dma((4, nf)), dma((4, nf)),
             dma((3, chips)), dma((3, chips)), dma((3, chips, nf)), dma((3, chips, nf)),
@@ -684,7 +685,7 @@
         out_shape=(jax.ShapeDtypeStruct((width, hid), F32), jax.ShapeDtypeStruct((1,), F32)),
         in_specs=[anywhere, vmem],
         out_specs=(anywhere, pl.BlockSpec(memory_space=pltpu.SMEM)),
-        scratch_shapes=[dma((4,))],
+        scratch_shapes=[full(width, hid), dma((2, 8))],
         compiler_params=pltpu.CompilerParams(vmem_limit_bytes=60 * 1024 * 1024),
         name="hand_out",
     )(vector, score)

time: 190 us -> 61.4 us (0.32)
  Pallas kernels: 188 us -> 59.9 us
    pallas_call x1, Pallas kernels: 129 us -> 4.77 us  [spread_call(): pl.pallas_call(hand_out, out_shape=(jax.ShapeDtypeStruct((width, hid), F3...]
    pallas_call x1, Pallas kernels: 58.9 us -> 55.1 us  [spread_call(): pl.pallas_call(functools.partial(spread, nf, nd), out_shape=(jax.ShapeDty...]
where the time goes in v5:
time: 61.4 us; the launch traced here: 61.1 us
  Pallas kernels  59.9 us (98%)
  between operations  1.29 us (2%)
    pallas_call x1, Pallas kernels, spread_call(): pl.pallas_call(functools.partial(spread, nf, nd), out_shape=(jax.ShapeDty...  55.1 us
    pallas_call x1, Pallas kernels, spread_call(): pl.pallas_call(hand_out, out_shape=(jax.ShapeDtypeStruct((width, hid), F3...  4.77 us

profile of v5, /device:TPU:0, one launch (start us, length us, event | category | flops | bytes accessed | tf_op | source)
XLA Modules:
  0.0 61.1 jit_solution(7234536181828361583)
XLA Ops:
  1.3 55.1 %lissa.1 = (f32[1024,1024]{1,0:T(8,128)}, f32[8,128]{1,0:T(8,128)}) custom-call(bf16[16,1024]{1,0:T(8,128)(2,1)} %noise_h.1, bf16[16,1024]{1,0:T(8,128)(2,1)} %action_h.1, bf16[2,1,256,256]{3,2,1,0:T(8,128)(2,1)} %kv_h.1, s32[1]{0:T(128)S(6)} %copy.10.flow, s32[1,16]{1,0:T(1,128)} %bitcast.1, bf16[1024,1024]{1,0:T(8,128)(2,1)} %w_up_h.1, ...), custom_call_target="tpu_custom_call" | custom-call | tf_op jit(solution)/shard_map/lissa/pallas_call | solution.py:661
  56.4 4.8 %hand_out.1 = (f32[1024,1024]{1,0:T(8,128)}, f32[1]{0:T(128)}) custom-call(f32[1024,1024]{1,0:T(8,128)} %get-tuple-element.4.held, f32[8,128]{1,0:T(8,128)} %get-tuple-element.5.tally), custom_call_target="tpu_custom_call" | custom-call | tf_op jit(solution)/shard_map/hand_out/pallas_call | solution.py:683

commit v6 on v5

--- a/solution.py
+++ b/solution.py
@@ -623,27 +623,6 @@
     score[...] = -value / (acts * math.sqrt(width * hid * nf))
     for copy in sent:
         copy.wait_send()
-    for store in stores:
-        store.wait()
-
-
-def hand_out(held, tally, out, score, stage, sems):
-    parts = sems.shape[1]
-    high = out.shape[0] // parts
-
-    def move(i, to):
-        at = pl.ds(i * high, high)
-        src, dst = (stage, out) if to else (held, stage)
-        return pltpu.make_async_copy(src.at[at, :], dst.at[at, :], sems.at[to, i])
-
-    loads = [move(i, 0) for i in range(parts)]
-    stores = [move(i, 1) for i in range(parts)]
-    for load in loads:
-        load.start()
-    score[0] = tally[0, 0]
-    for load, store in zip(loads, stores):
-        load.wait()
-        store.start()
     for store in stores:
         store.wait()
 
@@ -676,19 +655,11 @@
             dma((3, chips)), dma((3, chips)),
         ],
         compiler_params=pltpu.CompilerParams(
-            collective_id=0, has_side_effects=True, vmem_limit_bytes=60 * 1024 * 1024
+            collective_id=0, has_side_effects=True, vmem_limit_bytes=44 * 1024 * 1024
         ),
         name="lissa",
     )(noise, action, kv, flow, mask.reshape(1, acts), w_up, w_down, grad)
-    return pl.pallas_call(
-        hand_out,
-        out_shape=(jax.ShapeDtypeStruct((width, hid), F32), jax.ShapeDtypeStruct((1,), F32)),
-        in_specs=[anywhere, vmem],
-        out_specs=(anywhere, pl.BlockSpec(memory_space=pltpu.SMEM)),
-        scratch_shapes=[full(width, hid), dma((2, 8))],
-        compiler_params=pltpu.CompilerParams(vmem_limit_bytes=60 * 1024 * 1024),
-        name="hand_out",
-    )(vector, score)
+    return vector, score[0, 0:1]
 
 
 def finish(total, every, mix, grad, out):

time: 61.4 us -> 65 us (1.059)
  local copies, waits for them, and re-layouts: 0 us -> 8.82 us
  Pallas kernels: 59.9 us -> 54.5 us
    unnamed x0 -> x13, local copies, waits for them, and re-layouts: none -> 8.31 us
    pallas_call x1 -> x0, Pallas kernels: 4.77 us -> none  [spread_call(): pl.pallas_call(hand_out, out_shape=(jax.ShapeDtypeStruct((width, hid), F3...]
where the time goes in v6:
time: 65 us; the launch traced here: 64.7 us
  Pallas kernels  54.5 us (84%)
  local copies, waits for them, and re-layouts  8.82 us (14%)
  between operations  1.3 us (2%)
    pallas_call x1, Pallas kernels, spread_call(): pl.pallas_call(functools.partial(spread, nf, nd), out_shape=(jax.ShapeDty...  54.5 us
    unnamed x13, local copies, waits for them, and re-layouts  8.31 us

profile of v6, /device:TPU:0, one launch (start us, length us, event | category | flops | bytes accessed | tf_op | source)
XLA Modules:
  0.0 64.7 jit_solution(16678124718883115916)
XLA Ops:
  1.3 0.0 copy-start
  1.3 1.6 %copy-done = bf16[1024,1024]{1,0:T(8,128)(2,1)S(1)} copy-done((bf16[1024,1024]{1,0:T(8,128)(2,1)S(1)}, bf16[1024,1024]{1,0:T(8,128)(2,1)}, u32[]{:S(2)}) %copy-start) | copy-done | bytes 2097176
  2.9 0.0 copy-start.1
  2.9 1.6 %copy-done.1 = bf16[1024,1024]{1,0:T(8,128)(2,1)S(1)} copy-done((bf16[1024,1024]{1,0:T(8,128)(2,1)S(1)}, bf16[1024,1024]{1,0:T(8,128)(2,1)}, u32[]{:S(2)}) %copy-start.1) | copy-done | bytes 2097176
  4.5 0.0 copy-start.2
  4.5 0.9 %copy-done.2 = bf16[2,1,256,256]{3,2,1,0:T(8,128)(2,1)S(1)} copy-done((bf16[2,1,256,256]{3,2,1,0:T(8,128)(2,1)S(1)}, bf16[2,1,256,256]{3,2,1,0:T(8,128)(2,1)}, u32[]{:S(2)}) %copy-start.2) | copy-done | bytes 262168
  5.4 0.0 copy-start.3
  5.4 0.8 %copy-done.3 = bf16[16,1024]{1,0:T(8,128)(2,1)S(1)} copy-done((bf16[16,1024]{1,0:T(8,128)(2,1)S(1)}, bf16[16,1024]{1,0:T(8,128)(2,1)}, u32[]{:S(2)}) %copy-start.3) | copy-done | bytes 32792
  6.2 0.0 copy-start.4
  6.2 0.8 %copy-done.4 = bf16[16,1024]{1,0:T(8,128)(2,1)S(1)} copy-done((bf16[16,1024]{1,0:T(8,128)(2,1)S(1)}, bf16[16,1024]{1,0:T(8,128)(2,1)}, u32[]{:S(2)}) %copy-start.4) | copy-done | bytes 32792
  6.9 0.0 copy-start.5
  6.9 0.7 %copy-done.5 = s32[16]{0:T(128)S(1)} copy-done((s32[16]{0:T(128)S(1)}, s32[16]{0:T(128)}, u32[]{:S(2)}) %copy-start.5) | copy-done | bytes 88
  7.6 54.5 %lissa.1 = (f32[1024,1024]{1,0:T(8,128)S(1)}, f32[8,128]{1,0:T(8,128)S(1)}) custom-call(bf16[16,1024]{1,0:T(8,128)(2,1)S(1)} %copy-done.3, bf16[16,1024]{1,0:T(8,128)(2,1)S(1)} %copy-done.4, bf16[2,1,256,256]{3,2,1,0:T(8,128)(2,1)S(1)} %copy-done.2, s32[1]{0:T(128)S(6)} %copy.11.flow, s32[1,16]{1,0:T(1,128)S(1)} %bitcast.2, bf16[1024,1024]{1,0:T(8,128)(2,1)S(1)} %copy-done, ...), custom_call_target="tpu_custom_call" | custom-call | tf_op jit(solution)/shard_map/lissa/pallas_call | solution.py:640
  62.1 0.5 slice.3
  62.6 2.0 %copy.12 = f32[1024,1024]{1,0:T(8,128)} copy(f32[1024,1024]{1,0:T(8,128)S(1)} %get-tuple-element.8) | data formatting | bytes 8388608
Async XLA Ops:
  1.3 1.6 %copy-start = (bf16[1024,1024]{1,0:T(8,128)(2,1)S(1)}, bf16[1024,1024]{1,0:T(8,128)(2,1)}, u32[]{:S(2)}) copy-start(bf16[1024,1024]{1,0:T(8,128)(2,1)} %w_up_h.1) | copy-start | bytes 6291460
  2.9 1.6 %copy-start.1 = (bf16[1024,1024]{1,0:T(8,128)(2,1)S(1)}, bf16[1024,1024]{1,0:T(8,128)(2,1)}, u32[]{:S(2)}) copy-start(bf16[1024,1024]{1,0:T(8,128)(2,1)} %w_down_h.1) | copy-start | bytes 6291460
  4.5 0.9 %copy-start.2 = (bf16[2,1,256,256]{3,2,1,0:T(8,128)(2,1)S(1)}, bf16[2,1,256,256]{3,2,1,0:T(8,128)(2,1)}, u32[]{:S(2)}) copy-start(bf16[2,1,256,256]{3,2,1,0:T(8,128)(2,1)} %kv_h.1) | copy-start | bytes 786436
  5.4 0.8 %copy-start.3 = (bf16[16,1024]{1,0:T(8,128)(2,1)S(1)}, bf16[16,1024]{1,0:T(8,128)(2,1)}, u32[]{:S(2)}) copy-start(bf16[16,1024]{1,0:T(8,128)(2,1)} %noise_h.1) | copy-start | bytes 98308
  6.2 0.8 %copy-start.4 = (bf16[16,1024]{1,0:T(8,128)(2,1)S(1)}, bf16[16,1024]{1,0:T(8,128)(2,1)}, u32[]{:S(2)}) copy-start(bf16[16,1024]{1,0:T(8,128)(2,1)} %action_h.1) | copy-start | bytes 98308
  6.9 0.7 %copy-start.5 = (s32[16]{0:T(128)S(1)}, s32[16]{0:T(128)}, u32[]{:S(2)}) copy-start(s32[16]{0:T(128)} %param.12) | copy-start | bytes 196

commit v7 on v5

--- a/solution.py
+++ b/solution.py
@@ -613,8 +613,8 @@
     stores = []
     for i in range(width // wide):
         cut = pl.ds(i * wide, wide)
-        grad[cut, :] = grad[cut, :] - dot32(flipped[cut, :], seconds[1]) * (1.0 / total)
-        stores.append(pltpu.make_async_copy(grad.at[cut, :], out.at[cut, :], store_sem.at[i]))
+        gradb[cut, :] = (grad[cut, :] - dot32(flipped[cut, :], seconds[1]) * (1.0 / total)).astype(BF)
+        stores.append(pltpu.make_async_copy(gradb.at[cut, :], out.at[cut, :], store_sem.at[i]))
         stores[-1].start()
     value = tally[f]
     for k in range(1, nf):
@@ -627,13 +627,13 @@
         store.wait()
 
 
-def hand_out(held, tally, out, score, stage, sems):
+def hand_out(held, tally, out, score, taken, stage, sems):
     parts = sems.shape[1]
     high = out.shape[0] // parts
 
     def move(i, to):
         at = pl.ds(i * high, high)
-        src, dst = (stage, out) if to else (held, stage)
+        src, dst = (stage, out) if to else (held, taken)
         return pltpu.make_async_copy(src.at[at, :], dst.at[at, :], sems.at[to, i])
 
     loads = [move(i, 0) for i in range(parts)]
@@ -641,8 +641,10 @@
     for load in loads:
         load.start()
     score[0] = tally[0, 0]
-    for load, store in zip(loads, stores):
+    for i, (load, store) in enumerate(zip(loads, stores)):
         load.wait()
+        at = pl.ds(i * high, high)
+        stage[at, :] = taken[at, :].astype(F32)
         store.start()
     for store in stores:
         store.wait()
@@ -660,7 +662,7 @@
     half, full = (lambda *s: pltpu.VMEM(s, BF)), (lambda *s: pltpu.VMEM(s, F32))
     vector, score = pl.pallas_call(
         functools.partial(spread, nf, nd),
-        out_shape=(jax.ShapeDtypeStruct((width, hid), F32), jax.ShapeDtypeStruct((8, 128), F32)),
+        out_shape=(jax.ShapeDtypeStruct((width, hid), BF), jax.ShapeDtypeStruct((8, 128), F32)),
         in_specs=[anywhere] * 3 + [pl.BlockSpec(memory_space=pltpu.SMEM)] + [anywhere] * 4,
         out_specs=(anywhere, vmem),
         scratch_shapes=[
@@ -685,7 +687,7 @@
         out_shape=(jax.ShapeDtypeStruct((width, hid), F32), jax.ShapeDtypeStruct((1,), F32)),
         in_specs=[anywhere, vmem],
         out_specs=(anywhere, pl.BlockSpec(memory_space=pltpu.SMEM)),
-        scratch_shapes=[full(width, hid), dma((2, 8))],
+        scratch_shapes=[half(width, hid), full(width, hid), dma((2, 8))],
         compiler_params=pltpu.CompilerParams(vmem_limit_bytes=60 * 1024 * 1024),
         name="hand_out",
     )(vector, score)

time: 61.4 us -> 60.9 us (level)
  no operation moved by 1% of the time
where the time goes in v7:
time: 60.9 us; the launch traced here: 60.7 us
  Pallas kernels  59.4 us (98%)
  between operations  1.29 us (2%)
    pallas_call x1, Pallas kernels, spread_call(): pl.pallas_call(functools.partial(spread, nf, nd), out_shape=(jax.ShapeDty...  55.1 us
    pallas_call x1, Pallas kernels, spread_call(): pl.pallas_call(hand_out, out_shape=(jax.ShapeDtypeStruct((width, hid), F3...  4.31 us

profile of v7, /device:TPU:0, one launch (start us, length us, event | category | flops | bytes accessed | tf_op | source)
XLA Modules:
  0.0 60.7 jit_solution(4408100648209536318)
XLA Ops:
  1.3 55.1 %lissa.1 = (bf16[1024,1024]{1,0:T(8,128)(2,1)}, f32[8,128]{1,0:T(8,128)}) custom-call(bf16[16,1024]{1,0:T(8,128)(2,1)} %noise_h.1, bf16[16,1024]{1,0:T(8,128)(2,1)} %action_h.1, bf16[2,1,256,256]{3,2,1,0:T(8,128)(2,1)} %kv_h.1, s32[1]{0:T(128)S(6)} %copy.10.flow, s32[1,16]{1,0:T(1,128)} %bitcast.1, bf16[1024,1024]{1,0:T(8,128)(2,1)} %w_up_h.1, ...), custom_call_target="tpu_custom_call" | custom-call | tf_op jit(solution)/shard_map/lissa/pallas_call | solution.py:663
  56.4 4.3 %hand_out.1 = (f32[1024,1024]{1,0:T(8,128)}, f32[1]{0:T(128)}) custom-call(bf16[1024,1024]{1,0:T(8,128)(2,1)} %get-tuple-element.4.held, f32[8,128]{1,0:T(8,128)} %get-tuple-element.5.tally), custom_call_target="tpu_custom_call" | custom-call | tf_op jit(solution)/shard_map/hand_out/pallas_call | solution.py:685
